TPU v7x, 32 devices: a whole 2x2x4 slice. The times are simulated.
32 devices in a mesh: gx: 4 (over z), gy: 4 (over y, core), gz: 2 (over x).
Axes of the slice: x: 2, y: 2, z: 4, core: 2. Of those that a mesh axis runs over, the one named last changes fastest.
Arguments:
- solution: float32 [3, 32, 64, 256], P(None, 'gx', 'gy', 'gz'), may hold values from -6 to 6
- residual: float32 [3, 32, 64, 256], P(None, 'gx', 'gy', 'gz'), may hold values from -15 to 15
- density_bins: int32 [32, 64, 256], P('gx', 'gy', 'gz'), may hold values from 0 to 15
- fixed_dofs: int32 [3, 32, 64, 256], P(None, 'gx', 'gy', 'gz'), may hold values from 0 to 1
Outputs:
- solution_next: float32 [3, 32, 64, 256], P(None, 'gx', 'gy', 'gz')
- residual_next: float32 [3, 32, 64, 256], P(None, 'gx', 'gy', 'gz')
- direction: float32 [3, 32, 64, 256], P(None, 'gx', 'gy', 'gz')
All inputs are finite; a program needn't handle non-finite values.
Results may differ from a plain program's by a relative error of at most 0.0003.
Values sent between devices are 32-bit elements; how exact they have to be, the bound alone decides.
A program may use at most 64 MiB of HBM per device.

v0:
```python
import jax
import jax.numpy as jnp
from jax import lax
from jax.sharding import PartitionSpec as P

SWEEPS = 3
BINS = 16


damping = 0.6
eig_center = 1.05
eig_halfwidth = 0.95


def padded_2(cells, sides, width):
    for axis, dim in sides:
        count = lax.axis_size(axis)
        ends = count - 1
        head = lax.slice_in_dim(cells, 0, width, axis=dim)
        tail = lax.slice_in_dim(cells, cells.shape[dim] - width, cells.shape[dim], axis=dim)
        cells = jnp.concatenate(
            [
                lax.ppermute(tail, axis, [(i, (i + 1) % count) for i in range(ends)]),
                cells,
                lax.ppermute(head, axis, [((i + 1) % count, i) for i in range(ends)]),
            ],
            axis=dim,
        )
    return cells


def stiffness(density_bins):
    fraction = (density_bins.astype(jnp.float32) + 1.0) / BINS
    return 0.05 + 0.95 * fraction * fraction * fraction


def couplings(padded):
    center = padded[1:-1, 1:-1, 1:-1]

    def shared(other):
        return jnp.where(other > 0.0, 0.5 * (center + other), 0.0)

    upper = jnp.stack(
        [
            shared(padded[2:, 1:-1, 1:-1]),
            shared(padded[1:-1, 2:, 1:-1]),
            shared(padded[1:-1, 1:-1, 2:]),
        ]
    )
    lower = jnp.stack(
        [
            shared(padded[:-2, 1:-1, 1:-1]),
            shared(padded[1:-1, :-2, 1:-1]),
            shared(padded[1:-1, 1:-1, :-2]),
        ]
    )
    return (upper, lower)


def level_apply(field, padded, upper, lower, spring):
    total = spring * field
    total = (
        total
        + upper[0] * (field - padded[:, 2:, 1:-1, 1:-1])
        + lower[0] * (field - padded[:, :-2, 1:-1, 1:-1])
    )
    total = (
        total
        + upper[1] * (field - padded[:, 1:-1, 2:, 1:-1])
        + lower[1] * (field - padded[:, 1:-1, :-2, 1:-1])
    )
    total = (
        total
        + upper[2] * (field - padded[:, 1:-1, 1:-1, 2:])
        + lower[2] * (field - padded[:, 1:-1, 1:-1, :-2])
    )
    return total


def level_diagonal(upper, lower, spring):
    return jnp.sum(upper, axis=0) + jnp.sum(lower, axis=0) + spring


def restrict(field):
    channels, size_x, size_y, size_z = field.shape
    return field.reshape(channels, size_x // 2, 2, size_y // 2, 2, size_z // 2, 2).sum(
        axis=(2, 4, 6)
    )


def prolong(field):
    return jnp.repeat(jnp.repeat(jnp.repeat(field, 2, axis=1), 2, axis=2), 2, axis=3)


def coarse_links(links, offset):
    size_x, size_y, size_z = links.shape[1:]
    along_x = (
        links[0][offset::2].reshape(size_x // 2, size_y // 2, 2, size_z // 2, 2).sum(axis=(2, 4))
    )
    along_y = (
        links[1][:, offset::2].reshape(size_x // 2, 2, size_y // 2, size_z // 2, 2).sum(axis=(1, 4))
    )
    along_z = (
        links[2][:, :, offset::2]
        .reshape(size_x // 2, 2, size_y // 2, 2, size_z // 2)
        .sum(axis=(1, 3))
    )
    return jnp.stack([along_x, along_y, along_z])


def with_rim(field):
    return padded_2(field, (("gx", 1), ("gy", 2), ("gz", 3)), 1)


def chebyshev(rhs, upper, lower, spring, diagonal, padder):
    ratio = eig_center / eig_halfwidth
    factor = 1.0 / ratio
    update = rhs / (eig_center * diagonal)
    iterate = update
    for step_index in range(SWEEPS - 1):
        remainder = rhs - level_apply(iterate, padder(iterate), upper, lower, spring)
        next_factor = 1.0 / (2.0 * ratio - factor)
        update = (
            next_factor * factor * update + 2.0 * next_factor / eig_halfwidth * remainder / diagonal
        )
        iterate = iterate + update
        factor = next_factor
    return iterate


def shards(solution, residual, density_bins, fixed_dofs):
    fixed = fixed_dofs.astype(jnp.float32)
    free = 1.0 - fixed
    modulus = stiffness(density_bins)
    widened = padded_2(modulus[None], (("gx", 1), ("gy", 2), ("gz", 3)), 1)[0]
    fine_upper, fine_lower = couplings(widened)
    fine_spring = 0.1 * modulus
    fine_diag = free * level_diagonal(fine_upper, fine_lower, fine_spring) + fixed

    def fine_apply(field):
        masked = free * field
        return (
            free * level_apply(masked, with_rim(masked), fine_upper, fine_lower, fine_spring)
            + fixed * field
        )

    mid_upper = coarse_links(fine_upper, 1)
    mid_lower = coarse_links(fine_lower, 0)
    mid_spring = restrict(fine_spring[None])[0]
    mid_diag = level_diagonal(mid_upper, mid_lower, mid_spring)
    low_upper = coarse_links(mid_upper, 1)
    low_lower = coarse_links(mid_lower, 0)
    low_spring = restrict(mid_spring[None])[0]
    fine_corr = damping * residual / fine_diag
    mid_rhs = restrict(residual - fine_apply(fine_corr))
    mid_corr = damping * mid_rhs / mid_diag
    coarse_rhs = restrict(
        mid_rhs - level_apply(mid_corr, with_rim(mid_corr), mid_upper, mid_lower, mid_spring)
    )
    low_diag = level_diagonal(low_upper, low_lower, low_spring)
    coarse_corr = chebyshev(coarse_rhs, low_upper, low_lower, low_spring, low_diag, with_rim)
    mid_corr = mid_corr + prolong(coarse_corr)
    mid_corr = (
        mid_corr
        + damping
        * (mid_rhs - level_apply(mid_corr, with_rim(mid_corr), mid_upper, mid_lower, mid_spring))
        / mid_diag
    )
    fine_corr = fine_corr + prolong(mid_corr)
    direction = fine_corr + damping * (residual - fine_apply(fine_corr)) / fine_diag
    precond_inner = lax.psum(jnp.sum(residual * direction), ("gx", "gy", "gz"))
    image = fine_apply(direction)
    curve_inner = lax.psum(jnp.sum(direction * image), ("gx", "gy", "gz"))
    alpha = precond_inner / curve_inner
    return (solution + alpha * direction, residual - alpha * image, direction)


def solution(mesh):
    return jax.shard_map(
        shards,
        mesh=mesh,
        in_specs=(
            P(None, "gx", "gy", "gz"),
            P(None, "gx", "gy", "gz"),
            P("gx", "gy", "gz"),
            P(None, "gx", "gy", "gz"),
        ),
        out_specs=(P(None, "gx", "gy", "gz"), P(None, "gx", "gy", "gz"), P(None, "gx", "gy", "gz")),
        check_vma=False,
    )
```

profile of v0, /device:TPU:0, one launch (start us, length us, event | category | flops | bytes accessed | tf_op | source)
XLA Modules:
  0.0 292.8 jit_solution(14352904642668927399)
XLA Ops:
  2.8 5.6 %collective-permute-start = (f32[1,1,16,128]{3,2,1,0:T(8,128)S(1)}, f32[1,1,16,128]{3,2,1,0:T(8,128)S(1)}, u32[]{:S(2)}, u32[]{:S(2)}) collective-permute-start(f32[1,1,16,128]{3,2,1,0:T(8,128)S(1)} %get-tuple-element.74), channel_id=1, source_target_pairs={{0,8},{8,16},{16,24},{1,9},{9,17},{17,25},{2,10},{10,18},{18,26},{... | collective-permute-start | bytes 24584 | tf_op jit(solution)/shard_map/ppermute | solution.py:23
  16.3 4.6 %collective-permute-start.4 = (f32[1,10,18,1]{3,2,1,0:T(8,128)S(1)}, f32[1,10,18,1]{3,2,1,0:T(8,128)S(1)}, u32[]{:S(2)}, u32[]{:S(2)}) collective-permute-start(f32[1,10,18,1]{3,2,1,0:T(8,128)S(1)} %get-tuple-element.65), channel_id=1, source_target_pairs={{0,1},{2,3},{4,5},{6,7},{8,9},{10,11},{12,13},{14,15},{16,17},{18,... | collective-permute-start | bytes 2168 | tf_op jit(solution)/shard_map/ppermute | solution.py:23
  27.9 4.8 %collective-permute-start.7 = (f32[3,1,16,128]{3,2,1,0:T(8,128)S(1)}, f32[3,1,16,128]{3,2,1,0:T(8,128)S(1)}, u32[]{:S(2)}, u32[]{:S(2)}) collective-permute-start(f32[3,1,16,128]{3,2,1,0:T(8,128)S(1)} %get-tuple-element.55), channel_id=1, source_target_pairs={{0,8},{8,16},{16,24},{1,9},{9,17},{17,25},{2,10},{10,18},{18,26},{... | collective-permute-start | bytes 73736 | tf_op jit(solution)/shard_map/ppermute | solution.py:23
  35.6 3.0 %collective-permute-start.9 = (f32[3,10,1,128]{3,2,1,0:T(1,128)S(1)}, f32[3,10,1,128]{3,2,1,0:T(1,128)S(1)}, u32[]{:S(2)}, u32[]{:S(2)}) collective-permute-start(f32[3,10,1,128]{3,2,1,0:T(1,128)S(1)} %get-tuple-element.49), channel_id=1, source_target_pairs={{0,2},{2,4},{4,6},{1,3},{3,5},{5,7},{8,10},{10,12},{12,14},{9,11},... | collective-permute-start | bytes 46088 | tf_op jit(solution)/shard_map/ppermute | solution.py:23
  38.6 5.5 %reshape_broadcast_in_dim.3 = f32[4,2,8,2,64,2]{5,4,3,2,1,0:T(8,128)} reshape(f32[8,16,128]{2,1,0:T(8,128)S(1)} %get-tuple-element.73) | data formatting | bytes 131072 | tf_op jit(solution)/shard_map/reshape;broadcast_in_dim | solution.py:86
  53.6 4.4 %collective-permute-start.11 = (f32[3,10,18,1]{3,2,1,0:T(8,128)S(1)}, f32[3,10,18,1]{3,2,1,0:T(8,128)S(1)}, u32[]{:S(2)}, u32[]{:S(2)}) collective-permute-start(f32[3,10,18,1]{3,2,1,0:T(8,128)S(1)} %get-tuple-element.44), channel_id=1, source_target_pairs={{0,1},{2,3},{4,5},{6,7},{8,9},{10,11},{12,13},{14,15},{16,17},{18,... | collective-permute-start | bytes 6488 | tf_op jit(solution)/shard_map/ppermute | solution.py:23
  59.3 6.3 %collective-permute-done.11 = f32[3,10,18,1]{3,2,1,0:T(8,128)S(1)} collective-permute-done((f32[3,10,18,1]{3,2,1,0:T(8,128)S(1)}, f32[3,10,18,1]{3,2,1,0:T(8,128)S(1)}, u32[]{:S(2)}, u32[]{:S(2)}) %collective-permute-start.11) | collective-permute-done | bytes 2192 | tf_op jit(solution)/shard_map/ppermute | solution.py:23
  65.6 4.7 %collective-permute-done.10 = f32[3,10,18,1]{3,2,1,0:T(8,128)S(1)} collective-permute-done((f32[3,10,18,1]{3,2,1,0:T(8,128)S(1)}, f32[3,10,18,1]{3,2,1,0:T(8,128)S(1)}, u32[]{:S(2)}, u32[]{:S(2)}) %collective-permute-start.10) | collective-permute-done | bytes 2192 | tf_op jit(solution)/shard_map/ppermute | solution.py:25
  70.7 13.9 %reshape.191 = f32[3,4,2,8,2,64,2]{6,5,4,3,2,1,0:T(8,128)} reshape(f32[3,8,16,128]{3,2,1,0:T(8,128)S(1)} %fusion.49) | data formatting | bytes 393216 | tf_op jit(solution)/shard_map/reshape | solution.py:86
  84.7 5.5 %reduce_sum.262 = f32[3,4,8,64]{3,2,1,0:T(8,128)S(1)} reduce(f32[3,4,2,8,2,64,2]{6,5,4,3,2,1,0:T(8,128)} %reshape.191, f32[]{:T(128)} %constant.4.clone.1), dimensions={2,4,6}, to_apply=%region_0.1 | reduce | flops 43008 | bytes 221188 | tf_op jit(solution)/shard_map/reduce_sum | solution.py:86
  91.5 4.8 %collective-permute-start.13 = (f32[3,1,8,64]{3,2,1,0:T(8,128)S(1)}, f32[3,1,8,64]{3,2,1,0:T(8,128)S(1)}, u32[]{:S(2)}, u32[]{:S(2)}) collective-permute-start(f32[3,1,8,64]{3,2,1,0:T(8,128)S(1)} %get-tuple-element.82), channel_id=1, source_target_pairs={{0,8},{8,16},{16,24},{1,9},{9,17},{17,25},{2,10},{10,18},{18,26},{... | collective-permute-start | bytes 18440 | tf_op jit(solution)/shard_map/ppermute | solution.py:23
  104.4 3.1 %collective-permute-done.14 = f32[3,6,1,64]{3,2,1,0:T(1,128)S(1)} collective-permute-done((f32[3,6,1,64]{3,2,1,0:T(1,128)S(1)}, f32[3,6,1,64]{3,2,1,0:T(1,128)S(1)}, u32[]{:S(2)}, u32[]{:S(2)}) %collective-permute-start.14) | collective-permute-done | bytes 4640 | tf_op jit(solution)/shard_map/ppermute | solution.py:25
  108.9 4.6 %collective-permute-start.17 = (f32[3,6,10,1]{3,1,2,0:T(8,128)S(1)}, f32[3,6,10,1]{3,1,2,0:T(8,128)S(1)}, u32[]{:S(2)}, u32[]{:S(2)}) collective-permute-start(f32[3,6,10,1]{3,1,2,0:T(8,128)S(1)} %get-tuple-element.64), channel_id=1, source_target_pairs={{0,1},{2,3},{4,5},{6,7},{8,9},{10,11},{12,13},{14,15},{16,17},{18,... | collective-permute-start | bytes 2168 | tf_op jit(solution)/shard_map/ppermute | solution.py:23
  119.4 4.8 %collective-permute-start.19 = (f32[3,1,4,32]{3,2,1,0:T(4,128)S(1)}, f32[3,1,4,32]{3,2,1,0:T(4,128)S(1)}, u32[]{:S(2)}, u32[]{:S(2)}) collective-permute-start(f32[3,1,4,32]{3,2,1,0:T(4,128)S(1)} %get-tuple-element.90), channel_id=1, source_target_pairs={{0,8},{8,16},{16,24},{1,9},{9,17},{17,25},{2,10},{10,18},{18,26},{... | collective-permute-start | bytes 4616 | tf_op jit(solution)/shard_map/ppermute | solution.py:23
  130.8 4.4 %collective-permute-start.23 = (f32[3,4,6,1]{3,2,1,0:T(8,128)S(1)}, f32[3,4,6,1]{3,2,1,0:T(8,128)S(1)}, u32[]{:S(2)}, u32[]{:S(2)}) collective-permute-start(f32[3,4,6,1]{3,2,1,0:T(8,128)S(1)} %get-tuple-element.81), channel_id=1, source_target_pairs={{0,1},{2,3},{4,5},{6,7},{8,9},{10,11},{12,13},{14,15},{16,17},{18,... | collective-permute-start | bytes 872 | tf_op jit(solution)/shard_map/ppermute | solution.py:23
  136.9 4.3 %collective-permute-done.22 = f32[3,4,6,1]{3,2,1,0:T(8,128)S(1)} collective-permute-done((f32[3,4,6,1]{3,2,1,0:T(8,128)S(1)}, f32[3,4,6,1]{3,2,1,0:T(8,128)S(1)}, u32[]{:S(2)}, u32[]{:S(2)}) %collective-permute-start.22) | collective-permute-done | bytes 320 | tf_op jit(solution)/shard_map/ppermute | solution.py:25
  142.7 4.9 %collective-permute-start.25 = (f32[3,1,4,32]{3,2,1,0:T(4,128)S(1)}, f32[3,1,4,32]{3,2,1,0:T(4,128)S(1)}, u32[]{:S(2)}, u32[]{:S(2)}) collective-permute-start(f32[3,1,4,32]{3,2,1,0:T(4,128)S(1)} %get-tuple-element.88), channel_id=1, source_target_pairs={{0,8},{8,16},{16,24},{1,9},{9,17},{17,25},{2,10},{10,18},{18,26},{... | collective-permute-start | bytes 4616 | tf_op jit(solution)/shard_map/ppermute | solution.py:23
  157.4 4.3 %collective-permute-done.28 = f32[3,4,6,1]{3,2,1,0:T(8,128)S(1)} collective-permute-done((f32[3,4,6,1]{3,2,1,0:T(8,128)S(1)}, f32[3,4,6,1]{3,2,1,0:T(8,128)S(1)}, u32[]{:S(2)}, u32[]{:S(2)}) %collective-permute-start.28) | collective-permute-done | bytes 320 | tf_op jit(solution)/shard_map/ppermute | solution.py:25
  163.6 4.8 %collective-permute-start.31 = (f32[3,1,8,64]{3,2,1,0:T(8,128)S(1)}, f32[3,1,8,64]{3,2,1,0:T(8,128)S(1)}, u32[]{:S(2)}, u32[]{:S(2)}) collective-permute-start(f32[3,1,8,64]{3,2,1,0:T(8,128)S(1)} %get-tuple-element.76), channel_id=1, source_target_pairs={{0,8},{8,16},{16,24},{1,9},{9,17},{17,25},{2,10},{10,18},{18,26},{... | collective-permute-start | bytes 18440 | tf_op jit(solution)/shard_map/ppermute | solution.py:23
  169.8 3.1 %collective-permute-start.33 = (f32[3,6,1,64]{3,2,1,0:T(1,128)S(1)}, f32[3,6,1,64]{3,2,1,0:T(1,128)S(1)}, u32[]{:S(2)}, u32[]{:S(2)}) collective-permute-start(f32[3,6,1,64]{3,2,1,0:T(1,128)S(1)} %get-tuple-element.70), channel_id=1, source_target_pairs={{0,2},{2,4},{4,6},{1,3},{3,5},{5,7},{8,10},{10,12},{12,14},{9,11},... | collective-permute-start | bytes 13832 | tf_op jit(solution)/shard_map/ppermute | solution.py:23
  174.2 5.8 %collective-permute-done.32 = f32[3,6,1,64]{3,2,1,0:T(1,128)S(1)} collective-permute-done((f32[3,6,1,64]{3,2,1,0:T(1,128)S(1)}, f32[3,6,1,64]{3,2,1,0:T(1,128)S(1)}, u32[]{:S(2)}, u32[]{:S(2)}) %collective-permute-start.32) | collective-permute-done | bytes 4640 | tf_op jit(solution)/shard_map/ppermute | solution.py:25
  181.4 4.6 %collective-permute-start.35 = (f32[3,6,10,1]{3,1,2,0:T(8,128)S(1)}, f32[3,6,10,1]{3,1,2,0:T(8,128)S(1)}, u32[]{:S(2)}, u32[]{:S(2)}) collective-permute-start(f32[3,6,10,1]{3,1,2,0:T(8,128)S(1)} %get-tuple-element.60), channel_id=1, source_target_pairs={{0,1},{2,3},{4,5},{6,7},{8,9},{10,11},{12,13},{14,15},{16,17},{18,... | collective-permute-start | bytes 2168 | tf_op jit(solution)/shard_map/ppermute | solution.py:23
  191.1 4.8 %collective-permute-start.37 = (f32[3,1,16,128]{3,2,1,0:T(8,128)S(1)}, f32[3,1,16,128]{3,2,1,0:T(8,128)S(1)}, u32[]{:S(2)}, u32[]{:S(2)}) collective-permute-start(f32[3,1,16,128]{3,2,1,0:T(8,128)S(1)} %get-tuple-element.53), channel_id=1, source_target_pairs={{0,8},{8,16},{16,24},{1,9},{9,17},{17,25},{2,10},{10,18},{18,26},{... | collective-permute-start | bytes 73736 | tf_op jit(solution)/shard_map/ppermute | solution.py:23
  198.8 3.0 %collective-permute-start.39 = (f32[3,10,1,128]{3,2,1,0:T(1,128)S(1)}, f32[3,10,1,128]{3,2,1,0:T(1,128)S(1)}, u32[]{:S(2)}, u32[]{:S(2)}) collective-permute-start(f32[3,10,1,128]{3,2,1,0:T(1,128)S(1)} %get-tuple-element.47), channel_id=1, source_target_pairs={{0,2},{2,4},{4,6},{1,3},{3,5},{5,7},{8,10},{10,12},{12,14},{9,11},... | collective-permute-start | bytes 46088 | tf_op jit(solution)/shard_map/ppermute | solution.py:23
  202.9 4.5 %collective-permute-start.41 = (f32[3,10,18,1]{3,2,1,0:T(8,128)S(1)}, f32[3,10,18,1]{3,2,1,0:T(8,128)S(1)}, u32[]{:S(2)}, u32[]{:S(2)}) collective-permute-start(f32[3,10,18,1]{3,2,1,0:T(8,128)S(1)} %get-tuple-element.42), channel_id=1, source_target_pairs={{0,1},{2,3},{4,5},{6,7},{8,9},{10,11},{12,13},{14,15},{16,17},{18,... | collective-permute-start | bytes 6488 | tf_op jit(solution)/shard_map/ppermute | solution.py:23
  208.7 6.8 %collective-permute-done.41 = f32[3,10,18,1]{3,2,1,0:T(8,128)S(1)} collective-permute-done((f32[3,10,18,1]{3,2,1,0:T(8,128)S(1)}, f32[3,10,18,1]{3,2,1,0:T(8,128)S(1)}, u32[]{:S(2)}, u32[]{:S(2)}) %collective-permute-start.41) | collective-permute-done | bytes 2192 | tf_op jit(solution)/shard_map/ppermute | solution.py:23
  215.5 4.7 %collective-permute-done.40 = f32[3,10,18,1]{3,2,1,0:T(8,128)S(1)} collective-permute-done((f32[3,10,18,1]{3,2,1,0:T(8,128)S(1)}, f32[3,10,18,1]{3,2,1,0:T(8,128)S(1)}, u32[]{:S(2)}, u32[]{:S(2)}) %collective-permute-start.40) | collective-permute-done | bytes 2192 | tf_op jit(solution)/shard_map/ppermute | solution.py:25
  222.0 5.2 %collective-permute-start.43 = (f32[3,1,16,128]{3,2,1,0:T(8,128)S(1)}, f32[3,1,16,128]{3,2,1,0:T(8,128)S(1)}, u32[]{:S(2)}, u32[]{:S(2)}) collective-permute-start(f32[3,1,16,128]{3,2,1,0:T(8,128)S(1)} %get-tuple-element.51), channel_id=1, source_target_pairs={{0,8},{8,16},{16,24},{1,9},{9,17},{17,25},{2,10},{10,18},{18,26},{... | collective-permute-start | bytes 73736 | tf_op jit(solution)/shard_map/ppermute | solution.py:23
  230.0 3.0 %collective-permute-start.45 = (f32[3,10,1,128]{3,2,1,0:T(1,128)S(1)}, f32[3,10,1,128]{3,2,1,0:T(1,128)S(1)}, u32[]{:S(2)}, u32[]{:S(2)}) collective-permute-start(f32[3,10,1,128]{3,2,1,0:T(1,128)S(1)} %get-tuple-element.45), channel_id=1, source_target_pairs={{0,2},{2,4},{4,6},{1,3},{3,5},{5,7},{8,10},{10,12},{12,14},{9,11},... | collective-permute-start | bytes 46088 | tf_op jit(solution)/shard_map/ppermute | solution.py:23
  236.9 7.5 %collective-permute-done.47 = f32[3,10,18,1]{3,2,1,0:T(8,128)S(1)} collective-permute-done((f32[3,10,18,1]{3,2,1,0:T(8,128)S(1)}, f32[3,10,18,1]{3,2,1,0:T(8,128)S(1)}, u32[]{:S(2)}, u32[]{:S(2)}) %collective-permute-start.47) | collective-permute-done | bytes 2192 | tf_op jit(solution)/shard_map/ppermute | solution.py:23
  244.5 4.3 %collective-permute-done.46 = f32[3,10,18,1]{3,2,1,0:T(8,128)S(1)} collective-permute-done((f32[3,10,18,1]{3,2,1,0:T(8,128)S(1)}, f32[3,10,18,1]{3,2,1,0:T(8,128)S(1)}, u32[]{:S(2)}, u32[]{:S(2)}) %collective-permute-start.46) | collective-permute-done | bytes 2192 | tf_op jit(solution)/shard_map/ppermute | solution.py:25
  249.8 40.9 %all-reduce = (f32[]{:T(128)}, f32[]{:T(128)}) all-reduce(f32[]{:T(128)} %get-tuple-element.22, f32[]{:T(128)} %get-tuple-element.21), channel_id=1, replica_groups=mesh['gx'=4,'gy'=4,'gz'=2] {'gx','gy','gz'}, use_global_device_ids=true, to_apply=%region_17.18 | all-reduce | flops 2 | bytes 16 | tf_op jit(solution)/shard_map/psum | solution.py:171
  (186 shorter events, 93.0 us)
Async XLA Ops:
  1.5 6.9 %collective-permute-start.1 = (f32[1,1,16,128]{3,2,1,0:T(8,128)S(1)}, f32[1,1,16,128]{3,2,1,0:T(8,128)S(1)}, u32[]{:S(2)}, u32[]{:S(2)}) collective-permute-start(f32[1,1,16,128]{3,2,1,0:T(8,128)S(1)} %get-tuple-element.75), channel_id=1, source_target_pairs={{8,0},{16,8},{24,16},{9,1},{17,9},{25,17},{10,2},{18,10},{26,18},{... | collective-permute-start | bytes 24584 | tf_op jit(solution)/shard_map/ppermute | solution.py:25
  2.8 6.9 %collective-permute-start = (f32[1,1,16,128]{3,2,1,0:T(8,128)S(1)}, f32[1,1,16,128]{3,2,1,0:T(8,128)S(1)}, u32[]{:S(2)}, u32[]{:S(2)}) collective-permute-start(f32[1,1,16,128]{3,2,1,0:T(8,128)S(1)} %get-tuple-element.74), channel_id=1, source_target_pairs={{0,8},{8,16},{16,24},{1,9},{9,17},{17,25},{2,10},{10,18},{18,26},{... | collective-permute-start | bytes 24584 | tf_op jit(solution)/shard_map/ppermute | solution.py:23
  15.0 7.6 %collective-permute-start.5 = (f32[1,10,18,1]{3,2,1,0:T(8,128)S(1)}, f32[1,10,18,1]{3,2,1,0:T(8,128)S(1)}, u32[]{:S(2)}, u32[]{:S(2)}) collective-permute-start(f32[1,10,18,1]{3,2,1,0:T(8,128)S(1)} %get-tuple-element.66), channel_id=1, source_target_pairs={{1,0},{3,2},{5,4},{7,6},{9,8},{11,10},{13,12},{15,14},{17,16},{19,... | collective-permute-start | bytes 2168 | tf_op jit(solution)/shard_map/ppermute | solution.py:25
  16.3 8.0 %collective-permute-start.4 = (f32[1,10,18,1]{3,2,1,0:T(8,128)S(1)}, f32[1,10,18,1]{3,2,1,0:T(8,128)S(1)}, u32[]{:S(2)}, u32[]{:S(2)}) collective-permute-start(f32[1,10,18,1]{3,2,1,0:T(8,128)S(1)} %get-tuple-element.65), channel_id=1, source_target_pairs={{0,1},{2,3},{4,5},{6,7},{8,9},{10,11},{12,13},{14,15},{16,17},{18,... | collective-permute-start | bytes 2168 | tf_op jit(solution)/shard_map/ppermute | solution.py:23
  26.6 6.2 %collective-permute-start.6 = (f32[3,1,16,128]{3,2,1,0:T(8,128)S(1)}, f32[3,1,16,128]{3,2,1,0:T(8,128)S(1)}, u32[]{:S(2)}, u32[]{:S(2)}) collective-permute-start(f32[3,1,16,128]{3,2,1,0:T(8,128)S(1)} %get-tuple-element.56), channel_id=1, source_target_pairs={{8,0},{16,8},{24,16},{9,1},{17,9},{25,17},{10,2},{18,10},{26,18},{... | collective-permute-start | bytes 73736 | tf_op jit(solution)/shard_map/ppermute | solution.py:25
  27.9 6.4 %collective-permute-start.7 = (f32[3,1,16,128]{3,2,1,0:T(8,128)S(1)}, f32[3,1,16,128]{3,2,1,0:T(8,128)S(1)}, u32[]{:S(2)}, u32[]{:S(2)}) collective-permute-start(f32[3,1,16,128]{3,2,1,0:T(8,128)S(1)} %get-tuple-element.55), channel_id=1, source_target_pairs={{0,8},{8,16},{16,24},{1,9},{9,17},{17,25},{2,10},{10,18},{18,26},{... | collective-permute-start | bytes 73736 | tf_op jit(solution)/shard_map/ppermute | solution.py:23
  34.3 19.1 %collective-permute-start.8 = (f32[3,10,1,128]{3,2,1,0:T(1,128)S(1)}, f32[3,10,1,128]{3,2,1,0:T(1,128)S(1)}, u32[]{:S(2)}, u32[]{:S(2)}) collective-permute-start(f32[3,10,1,128]{3,2,1,0:T(1,128)S(1)} %get-tuple-element.50), channel_id=1, source_target_pairs={{2,0},{4,2},{6,4},{3,1},{5,3},{7,5},{10,8},{12,10},{14,12},{11,9},... | collective-permute-start | bytes 46088 | tf_op jit(solution)/shard_map/ppermute | solution.py:25
  35.6 17.8 %collective-permute-start.9 = (f32[3,10,1,128]{3,2,1,0:T(1,128)S(1)}, f32[3,10,1,128]{3,2,1,0:T(1,128)S(1)}, u32[]{:S(2)}, u32[]{:S(2)}) collective-permute-start(f32[3,10,1,128]{3,2,1,0:T(1,128)S(1)} %get-tuple-element.49), channel_id=1, source_target_pairs={{0,2},{2,4},{4,6},{1,3},{3,5},{5,7},{8,10},{10,12},{12,14},{9,11},... | collective-permute-start | bytes 46088 | tf_op jit(solution)/shard_map/ppermute | solution.py:23
  53.6 12.0 %collective-permute-start.11 = (f32[3,10,18,1]{3,2,1,0:T(8,128)S(1)}, f32[3,10,18,1]{3,2,1,0:T(8,128)S(1)}, u32[]{:S(2)}, u32[]{:S(2)}) collective-permute-start(f32[3,10,18,1]{3,2,1,0:T(8,128)S(1)} %get-tuple-element.44), channel_id=1, source_target_pairs={{0,1},{2,3},{4,5},{6,7},{8,9},{10,11},{12,13},{14,15},{16,17},{18,... | collective-permute-start | bytes 6488 | tf_op jit(solution)/shard_map/ppermute | solution.py:23
  58.0 12.4 %collective-permute-start.10 = (f32[3,10,18,1]{3,2,1,0:T(8,128)S(1)}, f32[3,10,18,1]{3,2,1,0:T(8,128)S(1)}, u32[]{:S(2)}, u32[]{:S(2)}) collective-permute-start(f32[3,10,18,1]{3,2,1,0:T(8,128)S(1)} %get-tuple-element.43), channel_id=1, source_target_pairs={{1,0},{3,2},{5,4},{7,6},{9,8},{11,10},{13,12},{15,14},{17,16},{19,... | collective-permute-start | bytes 6488 | tf_op jit(solution)/shard_map/ppermute | solution.py:25
  90.2 6.2 %collective-permute-start.12 = (f32[3,1,8,64]{3,2,1,0:T(8,128)S(1)}, f32[3,1,8,64]{3,2,1,0:T(8,128)S(1)}, u32[]{:S(2)}, u32[]{:S(2)}) collective-permute-start(f32[3,1,8,64]{3,2,1,0:T(8,128)S(1)} %get-tuple-element.83), channel_id=1, source_target_pairs={{8,0},{16,8},{24,16},{9,1},{17,9},{25,17},{10,2},{18,10},{26,18},{... | collective-permute-start | bytes 18440 | tf_op jit(solution)/shard_map/ppermute | solution.py:25
  91.5 6.2 %collective-permute-start.13 = (f32[3,1,8,64]{3,2,1,0:T(8,128)S(1)}, f32[3,1,8,64]{3,2,1,0:T(8,128)S(1)}, u32[]{:S(2)}, u32[]{:S(2)}) collective-permute-start(f32[3,1,8,64]{3,2,1,0:T(8,128)S(1)} %get-tuple-element.82), channel_id=1, source_target_pairs={{0,8},{8,16},{16,24},{1,9},{9,17},{17,25},{2,10},{10,18},{18,26},{... | collective-permute-start | bytes 18440 | tf_op jit(solution)/shard_map/ppermute | solution.py:23
  97.8 6.6 %collective-permute-start.15 = (f32[3,6,1,64]{3,2,1,0:T(1,128)S(1)}, f32[3,6,1,64]{3,2,1,0:T(1,128)S(1)}, u32[]{:S(2)}, u32[]{:S(2)}) collective-permute-start(f32[3,6,1,64]{3,2,1,0:T(1,128)S(1)} %get-tuple-element.72), channel_id=1, source_target_pairs={{0,2},{2,4},{4,6},{1,3},{3,5},{5,7},{8,10},{10,12},{12,14},{9,11},... | collective-permute-start | bytes 13832 | tf_op jit(solution)/shard_map/ppermute | solution.py:23
  107.6 6.8 %collective-permute-start.16 = (f32[3,6,10,1]{3,1,2,0:T(8,128)S(1)}, f32[3,6,10,1]{3,1,2,0:T(8,128)S(1)}, u32[]{:S(2)}, u32[]{:S(2)}) collective-permute-start(f32[3,6,10,1]{3,1,2,0:T(8,128)S(1)} %get-tuple-element.63), channel_id=1, source_target_pairs={{1,0},{3,2},{5,4},{7,6},{9,8},{11,10},{13,12},{15,14},{17,16},{19,... | collective-permute-start | bytes 2168 | tf_op jit(solution)/shard_map/ppermute | solution.py:25
  108.9 7.1 %collective-permute-start.17 = (f32[3,6,10,1]{3,1,2,0:T(8,128)S(1)}, f32[3,6,10,1]{3,1,2,0:T(8,128)S(1)}, u32[]{:S(2)}, u32[]{:S(2)}) collective-permute-start(f32[3,6,10,1]{3,1,2,0:T(8,128)S(1)} %get-tuple-element.64), channel_id=1, source_target_pairs={{0,1},{2,3},{4,5},{6,7},{8,9},{10,11},{12,13},{14,15},{16,17},{18,... | collective-permute-start | bytes 2168 | tf_op jit(solution)/shard_map/ppermute | solution.py:23
  118.1 6.1 %collective-permute-start.18 = (f32[3,1,4,32]{3,2,1,0:T(4,128)S(1)}, f32[3,1,4,32]{3,2,1,0:T(4,128)S(1)}, u32[]{:S(2)}, u32[]{:S(2)}) collective-permute-start(f32[3,1,4,32]{3,2,1,0:T(4,128)S(1)} %get-tuple-element.91), channel_id=1, source_target_pairs={{8,0},{16,8},{24,16},{9,1},{17,9},{25,17},{10,2},{18,10},{26,18},{... | collective-permute-start | bytes 4616 | tf_op jit(solution)/shard_map/ppermute | solution.py:25
  119.4 6.2 %collective-permute-start.19 = (f32[3,1,4,32]{3,2,1,0:T(4,128)S(1)}, f32[3,1,4,32]{3,2,1,0:T(4,128)S(1)}, u32[]{:S(2)}, u32[]{:S(2)}) collective-permute-start(f32[3,1,4,32]{3,2,1,0:T(4,128)S(1)} %get-tuple-element.90), channel_id=1, source_target_pairs={{0,8},{8,16},{16,24},{1,9},{9,17},{17,25},{2,10},{10,18},{18,26},{... | collective-permute-start | bytes 4616 | tf_op jit(solution)/shard_map/ppermute | solution.py:23
  141.4 6.2 %collective-permute-start.24 = (f32[3,1,4,32]{3,2,1,0:T(4,128)S(1)}, f32[3,1,4,32]{3,2,1,0:T(4,128)S(1)}, u32[]{:S(2)}, u32[]{:S(2)}) collective-permute-start(f32[3,1,4,32]{3,2,1,0:T(4,128)S(1)} %get-tuple-element.89), channel_id=1, source_target_pairs={{8,0},{16,8},{24,16},{9,1},{17,9},{25,17},{10,2},{18,10},{26,18},{... | collective-permute-start | bytes 4616 | tf_op jit(solution)/shard_map/ppermute | solution.py:25
  142.7 6.2 %collective-permute-start.25 = (f32[3,1,4,32]{3,2,1,0:T(4,128)S(1)}, f32[3,1,4,32]{3,2,1,0:T(4,128)S(1)}, u32[]{:S(2)}, u32[]{:S(2)}) collective-permute-start(f32[3,1,4,32]{3,2,1,0:T(4,128)S(1)} %get-tuple-element.88), channel_id=1, source_target_pairs={{0,8},{8,16},{16,24},{1,9},{9,17},{17,25},{2,10},{10,18},{18,26},{... | collective-permute-start | bytes 4616 | tf_op jit(solution)/shard_map/ppermute | solution.py:23
  162.3 6.1 %collective-permute-start.30 = (f32[3,1,8,64]{3,2,1,0:T(8,128)S(1)}, f32[3,1,8,64]{3,2,1,0:T(8,128)S(1)}, u32[]{:S(2)}, u32[]{:S(2)}) collective-permute-start(f32[3,1,8,64]{3,2,1,0:T(8,128)S(1)} %get-tuple-element.77), channel_id=1, source_target_pairs={{8,0},{16,8},{24,16},{9,1},{17,9},{25,17},{10,2},{18,10},{26,18},{... | collective-permute-start | bytes 18440 | tf_op jit(solution)/shard_map/ppermute | solution.py:25
  163.6 6.2 %collective-permute-start.31 = (f32[3,1,8,64]{3,2,1,0:T(8,128)S(1)}, f32[3,1,8,64]{3,2,1,0:T(8,128)S(1)}, u32[]{:S(2)}, u32[]{:S(2)}) collective-permute-start(f32[3,1,8,64]{3,2,1,0:T(8,128)S(1)} %get-tuple-element.76), channel_id=1, source_target_pairs={{0,8},{8,16},{16,24},{1,9},{9,17},{17,25},{2,10},{10,18},{18,26},{... | collective-permute-start | bytes 18440 | tf_op jit(solution)/shard_map/ppermute | solution.py:23
  172.9 7.1 %collective-permute-start.32 = (f32[3,6,1,64]{3,2,1,0:T(1,128)S(1)}, f32[3,6,1,64]{3,2,1,0:T(1,128)S(1)}, u32[]{:S(2)}, u32[]{:S(2)}) collective-permute-start(f32[3,6,1,64]{3,2,1,0:T(1,128)S(1)} %get-tuple-element.69), channel_id=1, source_target_pairs={{2,0},{4,2},{6,4},{3,1},{5,3},{7,5},{10,8},{12,10},{14,12},{11,9},... | collective-permute-start | bytes 13832 | tf_op jit(solution)/shard_map/ppermute | solution.py:25
  180.1 6.8 %collective-permute-start.34 = (f32[3,6,10,1]{3,1,2,0:T(8,128)S(1)}, f32[3,6,10,1]{3,1,2,0:T(8,128)S(1)}, u32[]{:S(2)}, u32[]{:S(2)}) collective-permute-start(f32[3,6,10,1]{3,1,2,0:T(8,128)S(1)} %get-tuple-element.59), channel_id=1, source_target_pairs={{1,0},{3,2},{5,4},{7,6},{9,8},{11,10},{13,12},{15,14},{17,16},{19,... | collective-permute-start | bytes 2168 | tf_op jit(solution)/shard_map/ppermute | solution.py:25
  181.4 7.1 %collective-permute-start.35 = (f32[3,6,10,1]{3,1,2,0:T(8,128)S(1)}, f32[3,6,10,1]{3,1,2,0:T(8,128)S(1)}, u32[]{:S(2)}, u32[]{:S(2)}) collective-permute-start(f32[3,6,10,1]{3,1,2,0:T(8,128)S(1)} %get-tuple-element.60), channel_id=1, source_target_pairs={{0,1},{2,3},{4,5},{6,7},{8,9},{10,11},{12,13},{14,15},{16,17},{18,... | collective-permute-start | bytes 2168 | tf_op jit(solution)/shard_map/ppermute | solution.py:23
  189.8 6.1 %collective-permute-start.36 = (f32[3,1,16,128]{3,2,1,0:T(8,128)S(1)}, f32[3,1,16,128]{3,2,1,0:T(8,128)S(1)}, u32[]{:S(2)}, u32[]{:S(2)}) collective-permute-start(f32[3,1,16,128]{3,2,1,0:T(8,128)S(1)} %get-tuple-element.54), channel_id=1, source_target_pairs={{8,0},{16,8},{24,16},{9,1},{17,9},{25,17},{10,2},{18,10},{26,18},{... | collective-permute-start | bytes 73736 | tf_op jit(solution)/shard_map/ppermute | solution.py:25
  191.1 6.3 %collective-permute-start.37 = (f32[3,1,16,128]{3,2,1,0:T(8,128)S(1)}, f32[3,1,16,128]{3,2,1,0:T(8,128)S(1)}, u32[]{:S(2)}, u32[]{:S(2)}) collective-permute-start(f32[3,1,16,128]{3,2,1,0:T(8,128)S(1)} %get-tuple-element.53), channel_id=1, source_target_pairs={{0,8},{8,16},{16,24},{1,9},{9,17},{17,25},{2,10},{10,18},{18,26},{... | collective-permute-start | bytes 73736 | tf_op jit(solution)/shard_map/ppermute | solution.py:23
  202.9 12.6 %collective-permute-start.41 = (f32[3,10,18,1]{3,2,1,0:T(8,128)S(1)}, f32[3,10,18,1]{3,2,1,0:T(8,128)S(1)}, u32[]{:S(2)}, u32[]{:S(2)}) collective-permute-start(f32[3,10,18,1]{3,2,1,0:T(8,128)S(1)} %get-tuple-element.42), channel_id=1, source_target_pairs={{0,1},{2,3},{4,5},{6,7},{8,9},{10,11},{12,13},{14,15},{16,17},{18,... | collective-permute-start | bytes 6488 | tf_op jit(solution)/shard_map/ppermute | solution.py:23
  207.3 12.9 %collective-permute-start.40 = (f32[3,10,18,1]{3,2,1,0:T(8,128)S(1)}, f32[3,10,18,1]{3,2,1,0:T(8,128)S(1)}, u32[]{:S(2)}, u32[]{:S(2)}) collective-permute-start(f32[3,10,18,1]{3,2,1,0:T(8,128)S(1)} %get-tuple-element.41), channel_id=1, source_target_pairs={{1,0},{3,2},{5,4},{7,6},{9,8},{11,10},{13,12},{15,14},{17,16},{19,... | collective-permute-start | bytes 6488 | tf_op jit(solution)/shard_map/ppermute | solution.py:25
  220.7 6.5 %collective-permute-start.42 = (f32[3,1,16,128]{3,2,1,0:T(8,128)S(1)}, f32[3,1,16,128]{3,2,1,0:T(8,128)S(1)}, u32[]{:S(2)}, u32[]{:S(2)}) collective-permute-start(f32[3,1,16,128]{3,2,1,0:T(8,128)S(1)} %get-tuple-element.52), channel_id=1, source_target_pairs={{8,0},{16,8},{24,16},{9,1},{17,9},{25,17},{10,2},{18,10},{26,18},{... | collective-permute-start | bytes 73736 | tf_op jit(solution)/shard_map/ppermute | solution.py:25
  222.0 6.7 %collective-permute-start.43 = (f32[3,1,16,128]{3,2,1,0:T(8,128)S(1)}, f32[3,1,16,128]{3,2,1,0:T(8,128)S(1)}, u32[]{:S(2)}, u32[]{:S(2)}) collective-permute-start(f32[3,1,16,128]{3,2,1,0:T(8,128)S(1)} %get-tuple-element.51), channel_id=1, source_target_pairs={{0,8},{8,16},{16,24},{1,9},{9,17},{17,25},{2,10},{10,18},{18,26},{... | collective-permute-start | bytes 73736 | tf_op jit(solution)/shard_map/ppermute | solution.py:23
  234.1 10.3 %collective-permute-start.47 = (f32[3,10,18,1]{3,2,1,0:T(8,128)S(1)}, f32[3,10,18,1]{3,2,1,0:T(8,128)S(1)}, u32[]{:S(2)}, u32[]{:S(2)}) collective-permute-start(f32[3,10,18,1]{3,2,1,0:T(8,128)S(1)} %get-tuple-element.40), channel_id=1, source_target_pairs={{0,1},{2,3},{4,5},{6,7},{8,9},{10,11},{12,13},{14,15},{16,17},{18,... | collective-permute-start | bytes 6488 | tf_op jit(solution)/shard_map/ppermute | solution.py:23
  235.6 13.2 %collective-permute-start.46 = (f32[3,10,18,1]{3,2,1,0:T(8,128)S(1)}, f32[3,10,18,1]{3,2,1,0:T(8,128)S(1)}, u32[]{:S(2)}, u32[]{:S(2)}) collective-permute-start(f32[3,10,18,1]{3,2,1,0:T(8,128)S(1)} %get-tuple-element.39), channel_id=1, source_target_pairs={{1,0},{3,2},{5,4},{7,6},{9,8},{11,10},{13,12},{15,14},{17,16},{19,... | collective-permute-start | bytes 6488 | tf_op jit(solution)/shard_map/ppermute | solution.py:25
  (20 other events, 275.1 us)
where the time goes:
time: 294 us; the launch traced here: 293 us
  starting transfers between devices  124 us (42%)
  waiting for transfers between devices  76.5 us (26%)
  blocking collectives  40.9 us (14%)
  local copies, waits for them, and re-layouts  29.7 us (10%)
  other arithmetic  18.6 us (6%)
  between operations  3.1 us (1%)
    ppermute x24, starting transfers between devices, padded_2(): lax.ppermute(tail, axis, [(i, (i + 1) % count) for i in range(ends)])  93 us
    ppermute x24, waiting for transfers between devices, padded_2(): lax.ppermute(tail, axis, [(i, (i + 1) % count) for i in range(ends)])  41.6 us
    psum x1, blocking collectives, shards(): precond_inner = lax.psum(jnp.sum(residual * direction), ('gx', 'gy', 'gz'))  40.9 us
    ppermute x24, waiting for transfers between devices, padded_2(): lax.ppermute(head, axis, [((i + 1) % count, i) for i in range(ends)])  34.9 us
    ppermute x24, starting transfers between devices, padded_2(): lax.ppermute(head, axis, [((i + 1) % count, i) for i in range(ends)])  31 us
    reshape x2, local copies, waits for them, and re-layouts, restrict(): field.reshape(channels, size_x // 2, 2, size_y // 2, 2, size_z // 2, 2)  15.5 us
    reduce_sum x4, other arithmetic, restrict(): field.reshape(channels, size_x // 2, 2, size_y // 2, 2, size_z // 2, 2)  8.36 us
    another operation x2, local copies, waits for them, and re-layouts, restrict(): field.reshape(channels, size_x // 2, 2, size_y // 2, 2, size_z // 2, 2)  6.05 us
  transfers between devices with their start and end apart: 48, of which 31 were waited for; matrix products, arithmetic and copies ran while one was open for 6% of the time, Pallas kernels for 0%

commit v1 on v0

v1 whole, which is shorter than its diff:
```python
import functools

import jax
import jax.numpy as jnp
from jax import lax
from jax.experimental import pallas as pl
from jax.experimental.pallas import tpu as pltpu
from jax.sharding import PartitionSpec as P

SWEEPS = 3
BINS = 16
AXES = ("gx", "gy", "gz")

damping = 0.6
eig_center = 1.05
eig_halfwidth = 0.95

ROUNDS = ("bins", 0, 1, 2, 2, 1, 0, 0)


def roll(v, shift, axis):
    shift = shift % v.shape[axis]
    return v if shift == 0 else pltpu.roll(v, shift, axis)


def iota(shape, dim):
    return lax.broadcasted_iota(jnp.int32, shape, dim)


def pair_sum(v, s, axis):
    even = (iota(v.shape, axis) // s) % 2 == 0
    return v + jnp.where(even, roll(v, -s, axis), roll(v, s, axis))


def restrict(v, s):
    lead = v.shape[:-3]
    nx, ny, nz = v.shape[-3:]
    w = v.reshape(lead + (nx // 2, 2, ny, nz))
    k = len(lead) + 1
    w = lax.index_in_dim(w, 0, k, False) + lax.index_in_dim(w, 1, k, False)
    return pair_sum(pair_sum(w, s, w.ndim - 2), s, w.ndim - 1)


def prolong(v):
    c, nx, ny, nz = v.shape
    return jnp.broadcast_to(v[:, :, None], (c, nx, 2, ny, nz)).reshape(c, 2 * nx, ny, nz)


def kernel(counts, sol, res, den, fix, out_s, out_r, out_d, *scratch):
    n_rounds = len(ROUNDS)
    bufs = [scratch[6 * r : 6 * r + 6] for r in range(n_rounds)]
    rest = scratch[6 * n_rounds :]
    coef = rest[0:3]
    free_ref, diag_ref, inv_ref, fc0_ref, inv1_ref, inv2_ref = rest[3:9]
    sums = rest[9:12]
    part, send_sem, recv_sem, ssend_sem, srecv_sem = rest[12:17]

    idx = [lax.axis_index(a) for a in AXES]
    ny, nz = den.shape[1:]
    half = ny // 2

    for r in range(n_rounds):
        _, xr, _, yr, _, zr = bufs[r]
        xr[...] = jnp.zeros_like(xr)
        yr[...] = jnp.zeros_like(yr)
        zr[...] = jnp.zeros_like(zr)

    barrier = pltpu.get_barrier_semaphore()
    for a, axis in enumerate(AXES):
        for k in range(1, counts[a]):
            pl.semaphore_signal(
                barrier,
                inc=1,
                device_id={axis: lax.rem(idx[a] + k, counts[a])},
                device_id_type=pl.DeviceIdType.MESH,
            )
    pl.semaphore_wait(barrier, sum(c - 1 for c in counts))

    def copies(r, a):
        field, xr, ys, yr, zs, zr = bufs[r]
        nx = field.shape[1]
        for up in (0, 1):
            if a == 0:
                src = field.at[:, pl.ds(0 if up else nx - 1, 1)]
                dst = xr.at[up]
            elif a == 1:
                src, dst = ys.at[up], yr.at[up]
            else:
                src, dst = zs, zr.at[up]
            slot = 2 * a + up
            yield pltpu.make_async_remote_copy(
                src_ref=src,
                dst_ref=dst,
                send_sem=send_sem.at[r, slot],
                recv_sem=recv_sem.at[r, slot],
                device_id={AXES[a]: idx[a] - 1 if up else idx[a] + 1},
                device_id_type=pl.DeviceIdType.MESH,
            )

    def has_next(a):
        return idx[a] < counts[a] - 1

    def has_prev(a):
        return idx[a] > 0

    def start(r, a):
        to_next, to_prev = copies(r, a)
        pl.when(has_next(a))(to_next.start)
        pl.when(has_prev(a))(to_prev.start)

    def wait(r, a):
        to_next, to_prev = copies(r, a)
        pl.when(has_prev(a))(to_next.wait_recv)
        pl.when(has_next(a))(to_prev.wait_recv)

    def send(r, v, s):
        field, xr, ys, yr, zs, zr = bufs[r]
        c, nx = v.shape[:2]
        field[...] = v
        start(r, 0)
        ys[0] = v[:, :, ny - 1 : ny]
        ys[1] = v[:, :, 0:1]
        start(r, 1)
        place = ((iota((ny, nz), 1) + s) % nz) // (2 * s)
        packed = jnp.zeros((ny, nz), jnp.float32)
        for p in range(c * nx):
            packed = jnp.where(place == p, roll(v[p // nx, p % nx], 2 * s * p, 1), packed)
        zs[...] = packed
        start(r, 2)

    def z_halo(r, s):
        field, _, _, _, _, zr = bufs[r]
        c, nx = field.shape[:2]
        wait(r, 2)
        even = (iota((ny, nz), 1) // s) % 2 == 0
        w = jnp.where(even, roll(zr[0], s, 1), roll(zr[1], -s, 1))
        planes = [roll(w, -2 * s * p, 1) for p in range(c * nx)]
        return jnp.stack(planes).reshape(c, nx, ny, nz)

    def set_coef(level, lows, ups):
        ref = coef[level]
        s = 2**level
        shape = lows[0].shape
        row, lane = iota(shape, 1), iota(shape, 2)
        zero = jnp.zeros(shape, jnp.float32)
        ref[0] = lows[0]
        ref[1] = ups[0]
        ref[2] = jnp.where(row >= s, lows[1], zero)
        ref[3] = jnp.where(row < ny - s, ups[1], zero)
        ref[4] = jnp.where(lane >= s, lows[2], zero)
        ref[5] = jnp.where(lane < nz - s, ups[2], zero)
        ref[6] = jnp.where(row < s, lows[1], jnp.where(row >= ny - s, ups[1], zero))
        ref[7] = jnp.where(lane < s, lows[2], jnp.where(lane >= nz - s, ups[2], zero))

    def local_sum(level, v):
        ref = coef[level]
        s = 2**level
        edge = jnp.zeros_like(v[:, :1])
        total = ref[0] * jnp.concatenate([edge, v[:, :-1]], 1)
        total = total + ref[1] * jnp.concatenate([v[:, 1:], edge], 1)
        total = total + ref[2] * roll(v, s, 2) + ref[3] * roll(v, -s, 2)
        return total + ref[4] * roll(v, s, 3) + ref[5] * roll(v, -s, 3)

    def halo_sum(level, r, total):
        ref = coef[level]
        s = 2**level
        _, xr, _, yr, _, _ = bufs[r]
        nx = total.shape[1]
        wait(r, 0)
        first = total[:, :1] + ref[0, 0:1] * xr[0]
        last = total[:, nx - 1 :] + ref[1, nx - 1 : nx] * xr[1]
        middle = [total[:, 1 : nx - 1]] if nx > 2 else []
        total = jnp.concatenate([first] + middle + [last], 1)
        wait(r, 1)
        top = total[:, :, :half] + ref[6, :, :half] * yr[0]
        bottom = total[:, :, half:] + ref[6, :, half:] * yr[1]
        total = jnp.concatenate([top, bottom], 2)
        return total + ref[7] * z_halo(r, s)

    def neighbours(level, r, v):
        send(r, v, 2**level)
        return halo_sum(level, r, local_sum(level, v))

    def coarse_links(level, lows, ups):
        s = 2**level
        nx = lows[0].shape[0]
        row = (iota(lows[0].shape, 1) // s) % 2
        lane = (iota(lows[0].shape, 2) // s) % 2

        def along_x(links, offset):
            w = links.reshape(nx // 2, 2, ny, nz)[:, offset]
            return pair_sum(pair_sum(w, s, 1), s, 2)

        low = [
            along_x(lows[0], 0),
            restrict(jnp.where(row == 0, lows[1], 0.0), s),
            restrict(jnp.where(lane == 0, lows[2], 0.0), s),
        ]
        up = [
            along_x(ups[0], 1),
            restrict(jnp.where(row == 1, ups[1], 0.0), s),
            restrict(jnp.where(lane == 1, ups[2], 0.0), s),
        ]
        return low, up

    def diagonal(lows, ups, spring):
        return lows[0] + lows[1] + lows[2] + ups[0] + ups[1] + ups[2] + spring

    fraction = (den[...].astype(jnp.float32) + 1.0) / BINS
    modulus = 0.05 + 0.95 * fraction * fraction * fraction
    send(0, modulus[None], 1)
    _, xr, _, yr, _, _ = bufs[0]
    row, lane = iota(modulus.shape, 1), iota(modulus.shape, 2)

    def shared(other):
        return jnp.where(other > 0.0, 0.5 * (modulus + other), 0.0)

    wait(0, 0)
    lows = [shared(jnp.concatenate([xr[0, 0], modulus[:-1]], 0))]
    ups = [shared(jnp.concatenate([modulus[1:], xr[1, 0]], 0))]
    wait(0, 1)
    lows.append(shared(jnp.where(row == 0, yr[0, 0], roll(modulus, 1, 1))))
    ups.append(shared(jnp.where(row == ny - 1, yr[1, 0], roll(modulus, -1, 1))))
    beside = z_halo(0, 1)[0]
    lows.append(shared(jnp.where(lane == 0, beside, roll(modulus, 1, 2))))
    ups.append(shared(jnp.where(lane == nz - 1, beside, roll(modulus, -1, 2))))
    spring = 0.1 * modulus

    fixed = fix[...].astype(jnp.float32)
    free_ref[...] = 1.0 - fixed
    diag_ref[...] = free_ref[...] * diagonal(lows, ups, spring) + fixed
    inv_ref[...] = 1.0 / diag_ref[...]
    fc0_ref[...] = damping * res[...] * inv_ref[...]

    masked = free_ref[...] * fc0_ref[...]
    send(1, masked, 1)
    set_coef(0, lows, ups)
    lows, ups = coarse_links(0, lows, ups)
    spring = restrict(spring, 1)
    set_coef(1, lows, ups)
    inv1_ref[...] = 1.0 / diagonal(lows, ups, spring)
    lows, ups = coarse_links(1, lows, ups)
    spring = restrict(spring, 2)
    set_coef(2, lows, ups)
    inv2_ref[...] = 1.0 / diagonal(lows, ups, spring)
    total = halo_sum(0, 1, local_sum(0, masked))
    mid_rhs = restrict((1.0 - damping) * res[...] + free_ref[...] * total, 1)
    mid0 = damping * mid_rhs * inv1_ref[...]
    scaled_rhs = restrict((1.0 - damping) * mid_rhs + neighbours(1, 2, mid0), 2) * inv2_ref[...]

    ratio = eig_center / eig_halfwidth
    factor = 1.0 / ratio
    update = scaled_rhs / eig_center
    iterate = update
    for step in range(SWEEPS - 1):
        remainder = scaled_rhs - iterate + neighbours(2, 3 + step, iterate) * inv2_ref[...]
        next_factor = 1.0 / (2.0 * ratio - factor)
        update = next_factor * factor * update + 2.0 * next_factor / eig_halfwidth * remainder
        iterate = iterate + update
        factor = next_factor

    mid = mid0 + prolong(iterate)
    mid = (1.0 - damping) * mid + mid0 + damping * neighbours(1, 5, mid) * inv1_ref[...]
    fine = fc0_ref[...] + prolong(mid)
    total = neighbours(0, 6, free_ref[...] * fine)
    direction = (
        (1.0 - damping) * fine + fc0_ref[...] + damping * free_ref[...] * total * inv_ref[...]
    )
    out_d[...] = direction
    total = neighbours(0, 7, free_ref[...] * direction)
    direction = out_d[...]
    image = diag_ref[...] * direction - free_ref[...] * total
    out_r[...] = image

    def fold(v):
        w = jnp.sum(v.reshape(-1, 8, nz), axis=0)
        return w + roll(w, 4, 0)

    tile = (8, nz)
    mine = jnp.where(iota(tile, 0) < 4, fold(res[...] * direction), fold(direction * image))

    sent = []
    for a in (2, 1, 0):
        buf = sums[a]
        part[a] = mine
        buf[idx[a]] = mine
        offsets = range(1, counts[a])
        hops = []
        for k in offsets:
            hops.append(
                pltpu.make_async_remote_copy(
                    src_ref=part.at[a],
                    dst_ref=buf.at[idx[a]],
                    send_sem=ssend_sem.at[a, k],
                    recv_sem=srecv_sem.at[a, k],
                    device_id={AXES[a]: lax.rem(idx[a] + k, counts[a])},
                    device_id_type=pl.DeviceIdType.MESH,
                )
            )
            hops[-1].start()
        for k in offsets:
            arrival = pltpu.make_async_remote_copy(
                src_ref=part.at[a],
                dst_ref=buf.at[lax.rem(idx[a] + counts[a] - k, counts[a])],
                send_sem=ssend_sem.at[a, k],
                recv_sem=srecv_sem.at[a, k],
                device_id={AXES[a]: lax.rem(idx[a] + k, counts[a])},
                device_id_type=pl.DeviceIdType.MESH,
            )
            arrival.wait_recv()
        mine = jnp.sum(buf[...], axis=0)
        sent += hops

    def grand(keep):
        picked = jnp.where(keep, mine, 0.0)
        return jnp.sum(jnp.sum(picked, axis=1, keepdims=True), axis=0, keepdims=True)

    head = iota(tile, 0) < 4
    alpha = grand(head) / grand(jnp.logical_not(head))
    out_s[...] = sol[...] + alpha * out_d[...]
    out_r[...] = res[...] - alpha * out_r[...]

    for hop in sent:
        hop.wait_send()
    for r in range(n_rounds):
        for a in range(3):
            to_next, to_prev = copies(r, a)
            pl.when(has_next(a))(to_next.wait_send)
            pl.when(has_prev(a))(to_prev.wait_send)


def shards(counts, solution, residual, density_bins, fixed_dofs):
    comps, nx, ny, nz = residual.shape
    f32 = jnp.float32
    scratch = []
    for level in ROUNDS:
        c, planes = (1, nx) if level == "bins" else (comps, nx // 2**level)
        scratch += [
            pltpu.VMEM((c, planes, ny, nz), f32),
            pltpu.VMEM((2, c, 1, ny, nz), f32),
            pltpu.VMEM((2, c, planes, 1, nz), f32),
            pltpu.VMEM((2, c, planes, 1, nz), f32),
            pltpu.VMEM((ny, nz), f32),
            pltpu.VMEM((2, ny, nz), f32),
        ]
    scratch += [pltpu.VMEM((8, nx // 2**level, ny, nz), f32) for level in range(3)]
    scratch += [pltpu.VMEM((comps, nx, ny, nz), f32)] * 4
    scratch += [pltpu.VMEM((nx // 2, ny, nz), f32), pltpu.VMEM((nx // 4, ny, nz), f32)]
    scratch += [pltpu.VMEM((c, 8, nz), f32) for c in counts]
    scratch += [
        pltpu.VMEM((3, 8, nz), f32),
        pltpu.SemaphoreType.DMA((len(ROUNDS), 6)),
        pltpu.SemaphoreType.DMA((len(ROUNDS), 6)),
        pltpu.SemaphoreType.DMA((3, max(counts))),
        pltpu.SemaphoreType.DMA((3, max(counts))),
    ]
    shape = jax.ShapeDtypeStruct(residual.shape, f32)
    return pl.pallas_call(
        functools.partial(kernel, counts),
        out_shape=(shape, shape, shape),
        in_specs=[pl.BlockSpec(memory_space=pltpu.VMEM)] * 4,
        out_specs=(pl.BlockSpec(memory_space=pltpu.VMEM),) * 3,
        scratch_shapes=scratch,
        compiler_params=pltpu.CompilerParams(
            collective_id=0, has_side_effects=True, vmem_limit_bytes=32 * 2**20
        ),
    )(solution, residual, density_bins, fixed_dofs)


def solution(mesh):
    counts = tuple(mesh.shape[a] for a in AXES)
    return jax.shard_map(
        functools.partial(shards, counts),
        mesh=mesh,
        in_specs=(P(None, *AXES), P(None, *AXES), P(*AXES), P(None, *AXES)),
        out_specs=(P(None, *AXES), P(None, *AXES), P(None, *AXES)),
        check_vma=False,
    )
```

time: 294 us -> 46.5 us (0.16)
  starting transfers between devices: 124 us -> 0 us
  waiting for transfers between devices: 76.5 us -> 0 us
  blocking collectives: 40.9 us -> 0 us
  Pallas kernels: 0 us -> 40 us
  local copies, waits for them, and re-layouts: 29.7 us -> 5.64 us
  other arithmetic: 18.6 us -> 0 us
    ppermute x48 -> x0, starting transfers between devices: 124 us -> none  [the longest x24 93 us: padded_2(): lax.ppermute(tail, axis, [(i, (i + 1) % count) for i in range(ends)])]
    ppermute x48 -> x0, waiting for transfers between devices: 76.5 us -> none  [the longest x24 41.6 us: padded_2(): lax.ppermute(tail, axis, [(i, (i + 1) % count) for i in range(ends)])]
    psum x1 -> x0, blocking collectives: 40.9 us -> none  [shards(): precond_inner = lax.psum(jnp.sum(residual * direction), ('gx', 'gy', 'gz'))]
    pallas_call x0 -> x1, Pallas kernels: none -> 40 us  [shards(): pl.pallas_call(functools.partial(kernel, counts), out_shape=(shape, shape...]
    reshape x6 -> x0, local copies, waits for them, and re-layouts: 16.6 us -> none  [the longest x2 15.5 us: restrict(): field.reshape(channels, size_x // 2, 2, size_y // 2, 2, size_z // 2, 2)]
    reduce_sum x17 -> x0, other arithmetic: 12.7 us -> none  [the longest x4 8.36 us: restrict(): field.reshape(channels, size_x // 2, 2, size_y // 2, 2, size_z // 2, 2)]
    another operation x2 -> x0, local copies, waits for them, and re-layouts: 6.05 us -> none  [restrict(): field.reshape(channels, size_x // 2, 2, size_y // 2, 2, size_z // 2, 2)]
    slice x34 -> x0, local copies, waits for them, and re-layouts: 5.9 us -> none  [the longest x4 2.69 us: coarse_links(): links[2][:, :, offset::2]]
  transfers between devices with their start and end apart: 48 -> 0, of which waited for: 31 -> 0; matrix products, arithmetic and copies ran while one was open for 6% -> 0% of each run, Pallas kernels for 0% -> 0%
where the time goes in v1:
time: 46.5 us; the launch traced here: 46.3 us
  Pallas kernels  40 us (86%)
  local copies, waits for them, and re-layouts  5.64 us (12%)
  between operations  0.65 us (1%)
    pallas_call x1, Pallas kernels, shards(): pl.pallas_call(functools.partial(kernel, counts), out_shape=(shape, shape...  40 us
    unnamed x11, local copies, waits for them, and re-layouts  5.64 us

profile of v1, /device:TPU:0, one launch (start us, length us, event | category | flops | bytes accessed | tf_op | source)
XLA Modules:
  0.0 46.3 jit_solution(9612153253766140992)
XLA Ops:
  0.6 0.0 copy-start
  0.6 0.9 %copy-done = f32[3,8,16,128]{3,2,1,0:T(8,128)S(1)} copy-done((f32[3,8,16,128]{3,2,1,0:T(8,128)S(1)}, f32[3,8,16,128]{3,2,1,0:T(8,128)}, u32[]{:S(2)}) %copy-start) | copy-done | bytes 196632
  1.6 0.0 copy-start.1
  1.6 0.9 %copy-done.1 = f32[3,8,16,128]{3,2,1,0:T(8,128)S(1)} copy-done((f32[3,8,16,128]{3,2,1,0:T(8,128)S(1)}, f32[3,8,16,128]{3,2,1,0:T(8,128)}, u32[]{:S(2)}) %copy-start.1) | copy-done | bytes 196632
  2.5 0.0 copy-start.2
  2.5 0.9 %copy-done.2 = s32[3,8,16,128]{3,2,1,0:T(8,128)S(1)} copy-done((s32[3,8,16,128]{3,2,1,0:T(8,128)S(1)}, s32[3,8,16,128]{3,2,1,0:T(8,128)}, u32[]{:S(2)}) %copy-start.2) | copy-done | bytes 196632
  3.4 0.0 copy-start.3
  3.4 0.8 %copy-done.3 = s32[8,16,128]{2,1,0:T(8,128)S(1)} copy-done((s32[8,16,128]{2,1,0:T(8,128)S(1)}, s32[8,16,128]{2,1,0:T(8,128)}, u32[]{:S(2)}) %copy-start.3) | copy-done | bytes 65560
  4.3 40.0 %shard_map.67 = (f32[3,8,16,128]{3,2,1,0:T(8,128)S(1)}, f32[3,8,16,128]{3,2,1,0:T(8,128)S(1)}, f32[3,8,16,128]{3,2,1,0:T(8,128)S(1)}) custom-call(f32[3,8,16,128]{3,2,1,0:T(8,128)S(1)} %copy-done, f32[3,8,16,128]{3,2,1,0:T(8,128)S(1)} %copy-done.1, s32[8,16,128]{2,1,0:T(8,128)S(1)} %copy-done.3, s32[3,8,16,128]{3,2,1,0:T(8,128)S(1)} %copy-done.2), custom_call_target="tpu_custom_call" | custom-call | tf_op jit(solution)/shard_map/pallas_call | solution.py:358
  44.3 0.7 %copy.10 = f32[3,8,16,128]{3,2,1,0:T(8,128)} copy(f32[3,8,16,128]{3,2,1,0:T(8,128)S(1)} %get-tuple-element.6) | data formatting | bytes 393216
  45.0 0.7 %copy.11 = f32[3,8,16,128]{3,2,1,0:T(8,128)} copy(f32[3,8,16,128]{3,2,1,0:T(8,128)S(1)} %get-tuple-element.7) | data formatting | bytes 393216
  45.6 0.7 %copy.12 = f32[3,8,16,128]{3,2,1,0:T(8,128)} copy(f32[3,8,16,128]{3,2,1,0:T(8,128)S(1)} %get-tuple-element.8) | data formatting | bytes 393216
Async XLA Ops:
  0.6 0.9 %copy-start = (f32[3,8,16,128]{3,2,1,0:T(8,128)S(1)}, f32[3,8,16,128]{3,2,1,0:T(8,128)}, u32[]{:S(2)}) copy-start(f32[3,8,16,128]{3,2,1,0:T(8,128)} %sol.1) | copy-start | bytes 589828
  1.6 0.9 %copy-start.1 = (f32[3,8,16,128]{3,2,1,0:T(8,128)S(1)}, f32[3,8,16,128]{3,2,1,0:T(8,128)}, u32[]{:S(2)}) copy-start(f32[3,8,16,128]{3,2,1,0:T(8,128)} %res.1) | copy-start | bytes 589828
  2.5 0.9 %copy-start.2 = (s32[3,8,16,128]{3,2,1,0:T(8,128)S(1)}, s32[3,8,16,128]{3,2,1,0:T(8,128)}, u32[]{:S(2)}) copy-start(s32[3,8,16,128]{3,2,1,0:T(8,128)} %fix.1) | copy-start | bytes 589828
  3.4 0.8 %copy-start.3 = (s32[8,16,128]{2,1,0:T(8,128)S(1)}, s32[8,16,128]{2,1,0:T(8,128)}, u32[]{:S(2)}) copy-start(s32[8,16,128]{2,1,0:T(8,128)} %den.1) | copy-start | bytes 196612

commit v2 on v1

--- a/solution.py
+++ b/solution.py
@@ -46,8 +46,17 @@
     return jnp.broadcast_to(v[:, :, None], (c, nx, 2, ny, nz)).reshape(c, 2 * nx, ny, nz)
 
 
-def kernel(counts, sol, res, den, fix, out_s, out_r, out_d, *scratch):
+def kernel(counts, sol_hbm, res_hbm, den_hbm, fix_hbm, out_s, out_r, out_d, *scratch):
     n_rounds = len(ROUNDS)
+    sol, res, den, fix, load_sem = scratch[-5:]
+    loads = [
+        pltpu.make_async_copy(src, dst, load_sem.at[i])
+        for i, (src, dst) in enumerate(
+            ((den_hbm, den), (res_hbm, res), (fix_hbm, fix), (sol_hbm, sol))
+        )
+    ]
+    for load in loads:
+        load.start()
     bufs = [scratch[6 * r : 6 * r + 6] for r in range(n_rounds)]
     rest = scratch[6 * n_rounds :]
     coef = rest[0:3]
@@ -58,12 +67,6 @@
     idx = [lax.axis_index(a) for a in AXES]
     ny, nz = den.shape[1:]
     half = ny // 2
-
-    for r in range(n_rounds):
-        _, xr, _, yr, _, zr = bufs[r]
-        xr[...] = jnp.zeros_like(xr)
-        yr[...] = jnp.zeros_like(yr)
-        zr[...] = jnp.zeros_like(zr)
 
     barrier = pltpu.get_barrier_semaphore()
     for a, axis in enumerate(AXES):
@@ -74,7 +77,15 @@
                 device_id={axis: lax.rem(idx[a] + k, counts[a])},
                 device_id_type=pl.DeviceIdType.MESH,
             )
-    pl.semaphore_wait(barrier, sum(c - 1 for c in counts))
+
+    for a in range(3):
+        for side, beyond in enumerate((idx[a] == 0, idx[a] == counts[a] - 1)):
+
+            @pl.when(beyond)
+            def _():
+                for r in range(n_rounds):
+                    ref = bufs[r][2 * a + 1]
+                    ref[side] = jnp.zeros(ref.shape[1:], jnp.float32)
 
     def copies(r, a):
         field, xr, ys, yr, zs, zr = bufs[r]
@@ -113,6 +124,12 @@
         pl.when(has_prev(a))(to_next.wait_recv)
         pl.when(has_next(a))(to_prev.wait_recv)
 
+    def sent_all(r):
+        for a in range(3):
+            to_next, to_prev = copies(r, a)
+            pl.when(has_next(a))(to_next.wait_send)
+            pl.when(has_prev(a))(to_prev.wait_send)
+
     def send(r, v, s):
         field, xr, ys, yr, zs, zr = bufs[r]
         c, nx = v.shape[:2]
@@ -166,6 +183,7 @@
         s = 2**level
         _, xr, _, yr, _, _ = bufs[r]
         nx = total.shape[1]
+        sent_all(r - 1)
         wait(r, 0)
         first = total[:, :1] + ref[0, 0:1] * xr[0]
         last = total[:, nx - 1 :] + ref[1, nx - 1 : nx] * xr[1]
@@ -206,8 +224,10 @@
     def diagonal(lows, ups, spring):
         return lows[0] + lows[1] + lows[2] + ups[0] + ups[1] + ups[2] + spring
 
+    loads[0].wait()
     fraction = (den[...].astype(jnp.float32) + 1.0) / BINS
     modulus = 0.05 + 0.95 * fraction * fraction * fraction
+    pl.semaphore_wait(barrier, sum(c - 1 for c in counts))
     send(0, modulus[None], 1)
     _, xr, _, yr, _, _ = bufs[0]
     row, lane = iota(modulus.shape, 1), iota(modulus.shape, 2)
@@ -226,6 +246,8 @@
     ups.append(shared(jnp.where(lane == nz - 1, beside, roll(modulus, -1, 2))))
     spring = 0.1 * modulus
 
+    loads[1].wait()
+    loads[2].wait()
     fixed = fix[...].astype(jnp.float32)
     free_ref[...] = 1.0 - fixed
     diag_ref[...] = free_ref[...] * diagonal(lows, ups, spring) + fixed
@@ -317,16 +339,13 @@
 
     head = iota(tile, 0) < 4
     alpha = grand(head) / grand(jnp.logical_not(head))
+    loads[3].wait()
     out_s[...] = sol[...] + alpha * out_d[...]
     out_r[...] = res[...] - alpha * out_r[...]
 
     for hop in sent:
         hop.wait_send()
-    for r in range(n_rounds):
-        for a in range(3):
-            to_next, to_prev = copies(r, a)
-            pl.when(has_next(a))(to_next.wait_send)
-            pl.when(has_prev(a))(to_prev.wait_send)
+    sent_all(n_rounds - 1)
 
 
 def shards(counts, solution, residual, density_bins, fixed_dofs):
@@ -353,18 +372,27 @@
         pltpu.SemaphoreType.DMA((len(ROUNDS), 6)),
         pltpu.SemaphoreType.DMA((3, max(counts))),
         pltpu.SemaphoreType.DMA((3, max(counts))),
+        pltpu.VMEM(solution.shape, f32),
+        pltpu.VMEM(residual.shape, f32),
+        pltpu.VMEM(density_bins.shape, jnp.int32),
+        pltpu.VMEM(fixed_dofs.shape, jnp.int32),
+        pltpu.SemaphoreType.DMA((4,)),
+    ]
+    operands = [
+        pltpu.with_memory_space_constraint(x, pltpu.HBM)
+        for x in (solution, residual, density_bins, fixed_dofs)
     ]
     shape = jax.ShapeDtypeStruct(residual.shape, f32)
     return pl.pallas_call(
         functools.partial(kernel, counts),
         out_shape=(shape, shape, shape),
-        in_specs=[pl.BlockSpec(memory_space=pltpu.VMEM)] * 4,
+        in_specs=[pl.BlockSpec(memory_space=pltpu.HBM)] * 4,
         out_specs=(pl.BlockSpec(memory_space=pltpu.VMEM),) * 3,
         scratch_shapes=scratch,
         compiler_params=pltpu.CompilerParams(
             collective_id=0, has_side_effects=True, vmem_limit_bytes=32 * 2**20
         ),
-    )(solution, residual, density_bins, fixed_dofs)
+    )(*operands)
 
 
 def solution(mesh):

time: 46.5 us -> 42.8 us (0.920)
  local copies, waits for them, and re-layouts: 5.64 us -> 2.03 us
    unnamed x11 -> x3, local copies, waits for them, and re-layouts: 5.64 us -> 2.03 us
where the time goes in v2:
time: 42.8 us; the launch traced here: 42.7 us
  Pallas kernels  40 us (93%)
  local copies, waits for them, and re-layouts  2.03 us (5%)
  between operations  0.64 us (1%)
    pallas_call x1, Pallas kernels, shards(): pl.pallas_call(functools.partial(kernel, counts), out_shape=(shape, shape...  40 us
    unnamed x3, local copies, waits for them, and re-layouts  2.03 us

profile of v2, /device:TPU:0, one launch (start us, length us, event | category | flops | bytes accessed | tf_op | source)
XLA Modules:
  0.0 42.7 jit_solution(892741812385454490)
XLA Ops:
  0.6 40.0 %shard_map.67 = (f32[3,8,16,128]{3,2,1,0:T(8,128)S(1)}, f32[3,8,16,128]{3,2,1,0:T(8,128)S(1)}, f32[3,8,16,128]{3,2,1,0:T(8,128)S(1)}) custom-call(f32[3,8,16,128]{3,2,1,0:T(8,128)} %sol_hbm.1, f32[3,8,16,128]{3,2,1,0:T(8,128)} %res_hbm.1, s32[8,16,128]{2,1,0:T(8,128)} %den_hbm.1, s32[3,8,16,128]{3,2,1,0:T(8,128)} %fix_hbm.1), custom_call_target="tpu_custom_call" | custom-call | tf_op jit(solution)/shard_map/pallas_call | solution.py:386
  40.6 0.7 %copy.10 = f32[3,8,16,128]{3,2,1,0:T(8,128)} copy(f32[3,8,16,128]{3,2,1,0:T(8,128)S(1)} %get-tuple-element.6) | data formatting | bytes 393216
  41.3 0.7 %copy.11 = f32[3,8,16,128]{3,2,1,0:T(8,128)} copy(f32[3,8,16,128]{3,2,1,0:T(8,128)S(1)} %get-tuple-element.7) | data formatting | bytes 393216
  42.0 0.7 %copy.12 = f32[3,8,16,128]{3,2,1,0:T(8,128)} copy(f32[3,8,16,128]{3,2,1,0:T(8,128)S(1)} %get-tuple-element.8) | data formatting | bytes 393216

commit v3 on v2

--- a/solution.py
+++ b/solution.py
@@ -44,6 +44,18 @@
 def prolong(v):
     c, nx, ny, nz = v.shape
     return jnp.broadcast_to(v[:, :, None], (c, nx, 2, ny, nz)).reshape(c, 2 * nx, ny, nz)
+
+
+def sum_groups(counts):
+    total = counts[0] * counts[1] * counts[2]
+    return ((0, 1, 2),) if total <= 64 else ((2,), (1,), (0,))
+
+
+def group_size(counts, group):
+    size = 1
+    for a in group:
+        size *= counts[a]
+    return size
 
 
 def kernel(counts, sol_hbm, res_hbm, den_hbm, fix_hbm, out_s, out_r, out_d, *scratch):
@@ -61,22 +73,37 @@
     rest = scratch[6 * n_rounds :]
     coef = rest[0:3]
     free_ref, diag_ref, inv_ref, fc0_ref, inv1_ref, inv2_ref = rest[3:9]
-    sums = rest[9:12]
-    part, send_sem, recv_sem, ssend_sem, srecv_sem = rest[12:17]
+    part, send_sem, recv_sem, ssend_sem, srecv_sem = rest[9:14]
+    sums = rest[14:-5]
+    groups = sum_groups(counts)
 
     idx = [lax.axis_index(a) for a in AXES]
     ny, nz = den.shape[1:]
     half = ny // 2
 
     barrier = pltpu.get_barrier_semaphore()
-    for a, axis in enumerate(AXES):
-        for k in range(1, counts[a]):
+
+
+    def partner(group, k):
+        there, place, left = {}, 0, abs(k)
+        for a in reversed(group):
+            step = left % counts[a]
+            left //= counts[a]
+            there[a] = lax.rem(idx[a] + (step if k > 0 else counts[a] - step), counts[a])
+        for a in group:
+            place = place * counts[a] + there[a]
+        return {AXES[a]: there[a] for a in group}, place
+
+    greeted = 0
+    for group in groups:
+        for k in range(1, group_size(counts, group)):
             pl.semaphore_signal(
                 barrier,
                 inc=1,
-                device_id={axis: lax.rem(idx[a] + k, counts[a])},
+                device_id=partner(group, k)[0],
                 device_id_type=pl.DeviceIdType.MESH,
             )
+            greeted += 1
 
     for a in range(3):
         for side, beyond in enumerate((idx[a] == 0, idx[a] == counts[a] - 1)):
@@ -91,7 +118,9 @@
         field, xr, ys, yr, zs, zr = bufs[r]
         nx = field.shape[1]
         for up in (0, 1):
-            if a == 0:
+            if a == 0 and ROUNDS[r] in (1, 2):
+                src, dst = field.at[0, up], xr.at[up, 0, 0]
+            elif a == 0:
                 src = field.at[:, pl.ds(0 if up else nx - 1, 1)]
                 dst = xr.at[up]
             elif a == 1:
@@ -130,10 +159,30 @@
             pl.when(has_next(a))(to_next.wait_send)
             pl.when(has_prev(a))(to_prev.wait_send)
 
+    def share(face):
+        slot = 2 * (iota(face.shape[1:], 0) % 2) + iota(face.shape[1:], 1) % 2
+        out = face[0]
+        for k in range(1, face.shape[0]):
+            out = jnp.where(slot == k, face[k], out)
+        return out
+
+    def unshare(plane, c):
+        row, lane = iota(plane.shape, 0) % 2, iota(plane.shape, 1) % 2
+        out = []
+        for k in range(c):
+            i, j = k // 2, k % 2
+            w = jnp.where(lane == j, plane, roll(plane, 1 - 2 * j, 1))
+            out.append(jnp.where(row == i, w, roll(w, 1 - 2 * i, 0)))
+        return jnp.stack(out)[:, None]
+
     def send(r, v, s):
         field, xr, ys, yr, zs, zr = bufs[r]
         c, nx = v.shape[:2]
-        field[...] = v
+        if s == 1:
+            field[...] = v
+        else:
+            field[0, 0] = share(v[:, nx - 1])
+            field[0, 1] = share(v[:, 0])
         start(r, 0)
         ys[0] = v[:, :, ny - 1 : ny]
         ys[1] = v[:, :, 0:1]
@@ -185,8 +234,9 @@
         nx = total.shape[1]
         sent_all(r - 1)
         wait(r, 0)
-        first = total[:, :1] + ref[0, 0:1] * xr[0]
-        last = total[:, nx - 1 :] + ref[1, nx - 1 : nx] * xr[1]
+        faces = xr if s == 1 else [unshare(xr[i, 0, 0], total.shape[0]) for i in (0, 1)]
+        first = total[:, :1] + ref[0, 0:1] * faces[0]
+        last = total[:, nx - 1 :] + ref[1, nx - 1 : nx] * faces[1]
         middle = [total[:, 1 : nx - 1]] if nx > 2 else []
         total = jnp.concatenate([first] + middle + [last], 1)
         wait(r, 1)
@@ -227,7 +277,7 @@
     loads[0].wait()
     fraction = (den[...].astype(jnp.float32) + 1.0) / BINS
     modulus = 0.05 + 0.95 * fraction * fraction * fraction
-    pl.semaphore_wait(barrier, sum(c - 1 for c in counts))
+    pl.semaphore_wait(barrier, greeted)
     send(0, modulus[None], 1)
     _, xr, _, yr, _, _ = bufs[0]
     row, lane = iota(modulus.shape, 1), iota(modulus.shape, 2)
@@ -295,56 +345,50 @@
     out_r[...] = image
 
     def fold(v):
-        w = jnp.sum(v.reshape(-1, 8, nz), axis=0)
-        return w + roll(w, 4, 0)
-
-    tile = (8, nz)
-    mine = jnp.where(iota(tile, 0) < 4, fold(res[...] * direction), fold(direction * image))
+        w = jnp.sum(jnp.sum(v.reshape(-1, 8, nz), axis=0), axis=0, keepdims=True)
+        return w + roll(w, nz // 2, 1)
+
+    head = iota((1, nz), 1) < nz // 2
+    mine = jnp.where(head, fold(res[...] * direction), fold(direction * image))
 
     sent = []
-    for a in (2, 1, 0):
-        buf = sums[a]
-        part[a] = mine
-        buf[idx[a]] = mine
-        offsets = range(1, counts[a])
-        hops = []
-        for k in offsets:
-            hops.append(
-                pltpu.make_async_remote_copy(
-                    src_ref=part.at[a],
-                    dst_ref=buf.at[idx[a]],
-                    send_sem=ssend_sem.at[a, k],
-                    recv_sem=srecv_sem.at[a, k],
-                    device_id={AXES[a]: lax.rem(idx[a] + k, counts[a])},
-                    device_id_type=pl.DeviceIdType.MESH,
-                )
-            )
-            hops[-1].start()
-        for k in offsets:
-            arrival = pltpu.make_async_remote_copy(
-                src_ref=part.at[a],
-                dst_ref=buf.at[lax.rem(idx[a] + counts[a] - k, counts[a])],
-                send_sem=ssend_sem.at[a, k],
-                recv_sem=srecv_sem.at[a, k],
-                device_id={AXES[a]: lax.rem(idx[a] + k, counts[a])},
+    for g, group in enumerate(groups):
+        buf = sums[g]
+        size = group_size(counts, group)
+        own = 0
+        for a in group:
+            own = own * counts[a] + idx[a]
+        part[g] = mine
+        buf[own] = mine
+
+        def hop(k, slot):
+            return pltpu.make_async_remote_copy(
+                src_ref=part.at[g],
+                dst_ref=buf.at[slot],
+                send_sem=ssend_sem.at[g, k],
+                recv_sem=srecv_sem.at[g, k],
+                device_id=partner(group, k)[0],
                 device_id_type=pl.DeviceIdType.MESH,
             )
-            arrival.wait_recv()
+
+        hops = [hop(k, own) for k in range(1, size)]
+        for h in hops:
+            h.start()
+        for k in range(1, size):
+            hop(k, partner(group, -k)[1]).wait_recv()
         mine = jnp.sum(buf[...], axis=0)
         sent += hops
 
     def grand(keep):
-        picked = jnp.where(keep, mine, 0.0)
-        return jnp.sum(jnp.sum(picked, axis=1, keepdims=True), axis=0, keepdims=True)
-
-    head = iota(tile, 0) < 4
+        return jnp.sum(jnp.where(keep, mine, 0.0), axis=1, keepdims=True)
+
     alpha = grand(head) / grand(jnp.logical_not(head))
     loads[3].wait()
     out_s[...] = sol[...] + alpha * out_d[...]
     out_r[...] = res[...] - alpha * out_r[...]
 
-    for hop in sent:
-        hop.wait_send()
+    for h in sent:
+        h.wait_send()
     sent_all(n_rounds - 1)
 
 
@@ -365,13 +409,16 @@
     scratch += [pltpu.VMEM((8, nx // 2**level, ny, nz), f32) for level in range(3)]
     scratch += [pltpu.VMEM((comps, nx, ny, nz), f32)] * 4
     scratch += [pltpu.VMEM((nx // 2, ny, nz), f32), pltpu.VMEM((nx // 4, ny, nz), f32)]
-    scratch += [pltpu.VMEM((c, 8, nz), f32) for c in counts]
+    sizes = [group_size(counts, g) for g in sum_groups(counts)]
     scratch += [
-        pltpu.VMEM((3, 8, nz), f32),
+        pltpu.VMEM((len(sizes), 1, nz), f32),
         pltpu.SemaphoreType.DMA((len(ROUNDS), 6)),
         pltpu.SemaphoreType.DMA((len(ROUNDS), 6)),
-        pltpu.SemaphoreType.DMA((3, max(counts))),
-        pltpu.SemaphoreType.DMA((3, max(counts))),
+        pltpu.SemaphoreType.DMA((len(sizes), max(sizes))),
+        pltpu.SemaphoreType.DMA((len(sizes), max(sizes))),
+    ]
+    scratch += [pltpu.VMEM((size, 1, nz), f32) for size in sizes]
+    scratch += [
         pltpu.VMEM(solution.shape, f32),
         pltpu.VMEM(residual.shape, f32),
         pltpu.VMEM(density_bins.shape, jnp.int32),

time: 42.8 us -> 39.5 us (0.923)
  Pallas kernels: 40 us -> 36.7 us
    pallas_call x1, Pallas kernels: 40 us -> 36.7 us  [shards(): pl.pallas_call(functools.partial(kernel, counts), out_shape=(shape, shape...]
where the time goes in v3:
time: 39.5 us; the launch traced here: 39.3 us
  Pallas kernels  36.7 us (93%)
  local copies, waits for them, and re-layouts  2.03 us (5%)
  between operations  0.64 us (2%)
    pallas_call x1, Pallas kernels, shards(): pl.pallas_call(functools.partial(kernel, counts), out_shape=(shape, shape...  36.7 us
    unnamed x3, local copies, waits for them, and re-layouts  2.03 us

profile of v3, /device:TPU:0, one launch (start us, length us, event | category | flops | bytes accessed | tf_op | source)
XLA Modules:
  0.0 39.3 jit_solution(8855159413257327269)
XLA Ops:
  0.6 36.7 %shard_map.67 = (f32[3,8,16,128]{3,2,1,0:T(8,128)S(1)}, f32[3,8,16,128]{3,2,1,0:T(8,128)S(1)}, f32[3,8,16,128]{3,2,1,0:T(8,128)S(1)}) custom-call(f32[3,8,16,128]{3,2,1,0:T(8,128)} %sol_hbm.1, f32[3,8,16,128]{3,2,1,0:T(8,128)} %res_hbm.1, s32[8,16,128]{2,1,0:T(8,128)} %den_hbm.1, s32[3,8,16,128]{3,2,1,0:T(8,128)} %fix_hbm.1), custom_call_target="tpu_custom_call" | custom-call | tf_op jit(solution)/shard_map/pallas_call | solution.py:433
  37.3 0.7 %copy.10 = f32[3,8,16,128]{3,2,1,0:T(8,128)} copy(f32[3,8,16,128]{3,2,1,0:T(8,128)S(1)} %get-tuple-element.6) | data formatting | bytes 393216
  38.0 0.7 %copy.11 = f32[3,8,16,128]{3,2,1,0:T(8,128)} copy(f32[3,8,16,128]{3,2,1,0:T(8,128)S(1)} %get-tuple-element.7) | data formatting | bytes 393216
  38.7 0.7 %copy.12 = f32[3,8,16,128]{3,2,1,0:T(8,128)} copy(f32[3,8,16,128]{3,2,1,0:T(8,128)S(1)} %get-tuple-element.8) | data formatting | bytes 393216

commit v4 on v3

--- a/solution.py
+++ b/solution.py
@@ -28,7 +28,8 @@
 
 
 def pair_sum(v, s, axis):
-    even = (iota(v.shape, axis) // s) % 2 == 0
+    shape = (1,) * (v.ndim - 2) + v.shape[-2:]
+    even = jnp.broadcast_to((iota(shape, axis) & s) == 0, v.shape)
     return v + jnp.where(even, roll(v, -s, axis), roll(v, s, axis))
 
 
@@ -115,14 +116,10 @@
                     ref[side] = jnp.zeros(ref.shape[1:], jnp.float32)
 
     def copies(r, a):
-        field, xr, ys, yr, zs, zr = bufs[r]
-        nx = field.shape[1]
+        xs, xr, ys, yr, zs, zr = bufs[r]
         for up in (0, 1):
-            if a == 0 and ROUNDS[r] in (1, 2):
-                src, dst = field.at[0, up], xr.at[up, 0, 0]
-            elif a == 0:
-                src = field.at[:, pl.ds(0 if up else nx - 1, 1)]
-                dst = xr.at[up]
+            if a == 0:
+                src, dst = xs.at[up], xr.at[up]
             elif a == 1:
                 src, dst = ys.at[up], yr.at[up]
             else:
@@ -176,13 +173,14 @@
         return jnp.stack(out)[:, None]
 
     def send(r, v, s):
-        field, xr, ys, yr, zs, zr = bufs[r]
+        xs, _, ys, _, zs, _ = bufs[r]
         c, nx = v.shape[:2]
         if s == 1:
-            field[...] = v
+            xs[0] = v[:, nx - 1]
+            xs[1] = v[:, 0]
         else:
-            field[0, 0] = share(v[:, nx - 1])
-            field[0, 1] = share(v[:, 0])
+            xs[0, 0] = share(v[:, nx - 1])
+            xs[1, 0] = share(v[:, 0])
         start(r, 0)
         ys[0] = v[:, :, ny - 1 : ny]
         ys[1] = v[:, :, 0:1]
@@ -194,11 +192,10 @@
         zs[...] = packed
         start(r, 2)
 
-    def z_halo(r, s):
-        field, _, _, _, _, zr = bufs[r]
-        c, nx = field.shape[:2]
+    def z_halo(r, s, c, nx):
+        zr = bufs[r][5]
         wait(r, 2)
-        even = (iota((ny, nz), 1) // s) % 2 == 0
+        even = (iota((ny, nz), 1) & s) == 0
         w = jnp.where(even, roll(zr[0], s, 1), roll(zr[1], -s, 1))
         planes = [roll(w, -2 * s * p, 1) for p in range(c * nx)]
         return jnp.stack(planes).reshape(c, nx, ny, nz)
@@ -206,9 +203,8 @@
     def set_coef(level, lows, ups):
         ref = coef[level]
         s = 2**level
-        shape = lows[0].shape
-        row, lane = iota(shape, 1), iota(shape, 2)
-        zero = jnp.zeros(shape, jnp.float32)
+        row, lane = iota((1, ny, nz), 1), iota((1, ny, nz), 2)
+        zero = 0.0
         ref[0] = lows[0]
         ref[1] = ups[0]
         ref[2] = jnp.where(row >= s, lows[1], zero)
@@ -234,7 +230,7 @@
         nx = total.shape[1]
         sent_all(r - 1)
         wait(r, 0)
-        faces = xr if s == 1 else [unshare(xr[i, 0, 0], total.shape[0]) for i in (0, 1)]
+        faces = [xr[i][:, None] if s == 1 else unshare(xr[i, 0], total.shape[0]) for i in (0, 1)]
         first = total[:, :1] + ref[0, 0:1] * faces[0]
         last = total[:, nx - 1 :] + ref[1, nx - 1 : nx] * faces[1]
         middle = [total[:, 1 : nx - 1]] if nx > 2 else []
@@ -243,7 +239,7 @@
         top = total[:, :, :half] + ref[6, :, :half] * yr[0]
         bottom = total[:, :, half:] + ref[6, :, half:] * yr[1]
         total = jnp.concatenate([top, bottom], 2)
-        return total + ref[7] * z_halo(r, s)
+        return total + ref[7] * z_halo(r, s, total.shape[0], nx)
 
     def neighbours(level, r, v):
         send(r, v, 2**level)
@@ -252,8 +248,8 @@
     def coarse_links(level, lows, ups):
         s = 2**level
         nx = lows[0].shape[0]
-        row = (iota(lows[0].shape, 1) // s) % 2
-        lane = (iota(lows[0].shape, 2) // s) % 2
+        row = iota((1, ny, nz), 1) & s
+        lane = iota((1, ny, nz), 2) & s
 
         def along_x(links, offset):
             w = links.reshape(nx // 2, 2, ny, nz)[:, offset]
@@ -266,8 +262,8 @@
         ]
         up = [
             along_x(ups[0], 1),
-            restrict(jnp.where(row == 1, ups[1], 0.0), s),
-            restrict(jnp.where(lane == 1, ups[2], 0.0), s),
+            restrict(jnp.where(row != 0, ups[1], 0.0), s),
+            restrict(jnp.where(lane != 0, ups[2], 0.0), s),
         ]
         return low, up
 
@@ -280,18 +276,18 @@
     pl.semaphore_wait(barrier, greeted)
     send(0, modulus[None], 1)
     _, xr, _, yr, _, _ = bufs[0]
-    row, lane = iota(modulus.shape, 1), iota(modulus.shape, 2)
+    row, lane = iota((1, ny, nz), 1), iota((1, ny, nz), 2)
 
     def shared(other):
         return jnp.where(other > 0.0, 0.5 * (modulus + other), 0.0)
 
     wait(0, 0)
-    lows = [shared(jnp.concatenate([xr[0, 0], modulus[:-1]], 0))]
-    ups = [shared(jnp.concatenate([modulus[1:], xr[1, 0]], 0))]
+    lows = [shared(jnp.concatenate([xr[0], modulus[:-1]], 0))]
+    ups = [shared(jnp.concatenate([modulus[1:], xr[1]], 0))]
     wait(0, 1)
     lows.append(shared(jnp.where(row == 0, yr[0, 0], roll(modulus, 1, 1))))
     ups.append(shared(jnp.where(row == ny - 1, yr[1, 0], roll(modulus, -1, 1))))
-    beside = z_halo(0, 1)[0]
+    beside = z_halo(0, 1, 1, modulus.shape[0])[0]
     lows.append(shared(jnp.where(lane == 0, beside, roll(modulus, 1, 2))))
     ups.append(shared(jnp.where(lane == nz - 1, beside, roll(modulus, -1, 2))))
     spring = 0.1 * modulus
@@ -307,18 +303,22 @@
     masked = free_ref[...] * fc0_ref[...]
     send(1, masked, 1)
     set_coef(0, lows, ups)
+    total = local_sum(0, masked)
     lows, ups = coarse_links(0, lows, ups)
     spring = restrict(spring, 1)
+    inv1_ref[...] = 1.0 / diagonal(lows, ups, spring)
+    total = halo_sum(0, 1, total)
+    mid_rhs = restrict((1.0 - damping) * res[...] + free_ref[...] * total, 1)
+    mid0 = damping * mid_rhs * inv1_ref[...]
+    send(2, mid0, 2)
     set_coef(1, lows, ups)
-    inv1_ref[...] = 1.0 / diagonal(lows, ups, spring)
+    total = local_sum(1, mid0)
     lows, ups = coarse_links(1, lows, ups)
     spring = restrict(spring, 2)
     set_coef(2, lows, ups)
     inv2_ref[...] = 1.0 / diagonal(lows, ups, spring)
-    total = halo_sum(0, 1, local_sum(0, masked))
-    mid_rhs = restrict((1.0 - damping) * res[...] + free_ref[...] * total, 1)
-    mid0 = damping * mid_rhs * inv1_ref[...]
-    scaled_rhs = restrict((1.0 - damping) * mid_rhs + neighbours(1, 2, mid0), 2) * inv2_ref[...]
+    total = halo_sum(1, 2, total)
+    scaled_rhs = restrict((1.0 - damping) * mid_rhs + total, 2) * inv2_ref[...]
 
     ratio = eig_center / eig_halfwidth
     factor = 1.0 / ratio
@@ -339,17 +339,22 @@
         (1.0 - damping) * fine + fc0_ref[...] + damping * free_ref[...] * total * inv_ref[...]
     )
     out_d[...] = direction
-    total = neighbours(0, 7, free_ref[...] * direction)
-    direction = out_d[...]
-    image = diag_ref[...] * direction - free_ref[...] * total
-    out_r[...] = image
+    masked = free_ref[...] * direction
+    send(7, masked, 1)
 
     def fold(v):
         w = jnp.sum(jnp.sum(v.reshape(-1, 8, nz), axis=0), axis=0, keepdims=True)
         return w + roll(w, nz // 2, 1)
 
+    precond = fold(res[...] * direction)
+    image = diag_ref[...] * direction
+    curve = fold(direction * image)
+    out_r[...] = image
+    total = halo_sum(0, 7, local_sum(0, masked)) * free_ref[...]
+    curve = curve - fold(out_d[...] * total)
+    out_r[...] = out_r[...] - total
     head = iota((1, nz), 1) < nz // 2
-    mine = jnp.where(head, fold(res[...] * direction), fold(direction * image))
+    mine = jnp.where(head, precond, curve)
 
     sent = []
     for g, group in enumerate(groups):
@@ -392,15 +397,25 @@
     sent_all(n_rounds - 1)
 
 
+def deliver(*refs):
+    sem = refs[-1]
+    moves = [pltpu.make_async_copy(refs[i], refs[3 + i], sem.at[i]) for i in range(3)]
+    for move in moves:
+        move.start()
+    for move in moves:
+        move.wait()
+
+
 def shards(counts, solution, residual, density_bins, fixed_dofs):
     comps, nx, ny, nz = residual.shape
     f32 = jnp.float32
     scratch = []
     for level in ROUNDS:
         c, planes = (1, nx) if level == "bins" else (comps, nx // 2**level)
+        face = 1 if level in (1, 2) else c
         scratch += [
-            pltpu.VMEM((c, planes, ny, nz), f32),
-            pltpu.VMEM((2, c, 1, ny, nz), f32),
+            pltpu.VMEM((2, face, ny, nz), f32),
+            pltpu.VMEM((2, face, ny, nz), f32),
             pltpu.VMEM((2, c, planes, 1, nz), f32),
             pltpu.VMEM((2, c, planes, 1, nz), f32),
             pltpu.VMEM((ny, nz), f32),
@@ -430,7 +445,7 @@
         for x in (solution, residual, density_bins, fixed_dofs)
     ]
     shape = jax.ShapeDtypeStruct(residual.shape, f32)
-    return pl.pallas_call(
+    results = pl.pallas_call(
         functools.partial(kernel, counts),
         out_shape=(shape, shape, shape),
         in_specs=[pl.BlockSpec(memory_space=pltpu.HBM)] * 4,
@@ -440,6 +455,13 @@
             collective_id=0, has_side_effects=True, vmem_limit_bytes=32 * 2**20
         ),
     )(*operands)
+    return pl.pallas_call(
+        deliver,
+        out_shape=(shape, shape, shape),
+        in_specs=[pl.BlockSpec(memory_space=pltpu.VMEM)] * 3,
+        out_specs=(pl.BlockSpec(memory_space=pltpu.HBM),) * 3,
+        scratch_shapes=[pltpu.SemaphoreType.DMA((3,))],
+    )(*results)
 
 
 def solution(mesh):

time: 39.5 us -> 41.4 us (1.048)
  Pallas kernels: 36.7 us -> 38.6 us
    pallas_call x0 -> x1, Pallas kernels: none -> 1.94 us  [shards(): pl.pallas_call(deliver, out_shape=(shape, shape, shape), in_specs=[pl.Blo...]
    unnamed x3 -> x6, local copies, waits for them, and re-layouts: 2.03 us -> 2.02 us
where the time goes in v4:
time: 41.4 us; the launch traced here: 41.2 us
  Pallas kernels  38.6 us (93%)
  local copies, waits for them, and re-layouts  2.02 us (5%)
  between operations  0.65 us (2%)
    pallas_call x1, Pallas kernels, shards(): pl.pallas_call(functools.partial(kernel, counts), out_shape=(shape, shape...  36.6 us
    unnamed x6, local copies, waits for them, and re-layouts  2.02 us
    pallas_call x1, Pallas kernels, shards(): pl.pallas_call(deliver, out_shape=(shape, shape, shape), in_specs=[pl.Blo...  1.94 us

profile of v4, /device:TPU:0, one launch (start us, length us, event | category | flops | bytes accessed | tf_op | source)
XLA Modules:
  0.0 41.2 jit_solution(16730264230498653731)
XLA Ops:
  0.6 36.6 %shard_map.67 = (f32[3,8,16,128]{3,2,1,0:T(8,128)S(1)}, f32[3,8,16,128]{3,2,1,0:T(8,128)S(1)}, f32[3,8,16,128]{3,2,1,0:T(8,128)S(1)}) custom-call(f32[3,8,16,128]{3,2,1,0:T(8,128)} %sol_hbm.1, f32[3,8,16,128]{3,2,1,0:T(8,128)} %res_hbm.1, s32[8,16,128]{2,1,0:T(8,128)} %den_hbm.1, s32[3,8,16,128]{3,2,1,0:T(8,128)} %fix_hbm.1), custom_call_target="tpu_custom_call" | custom-call | tf_op jit(solution)/shard_map/pallas_call | solution.py:448
  37.2 0.0 copy-start
  37.3 0.7 %copy-done = f32[3,8,16,128]{3,2,1,0:T(8,128)} copy-done((f32[3,8,16,128]{3,2,1,0:T(8,128)}, f32[3,8,16,128]{3,2,1,0:T(8,128)S(1)}, u32[]{:S(2)}) %copy-start) | copy-done | bytes 196632
  37.9 0.0 copy-start.1
  37.9 0.7 %copy-done.1 = f32[3,8,16,128]{3,2,1,0:T(8,128)} copy-done((f32[3,8,16,128]{3,2,1,0:T(8,128)}, f32[3,8,16,128]{3,2,1,0:T(8,128)S(1)}, u32[]{:S(2)}) %copy-start.1) | copy-done | bytes 196632
  38.6 0.0 copy-start.2
  38.6 0.7 %copy-done.2 = f32[3,8,16,128]{3,2,1,0:T(8,128)} copy-done((f32[3,8,16,128]{3,2,1,0:T(8,128)}, f32[3,8,16,128]{3,2,1,0:T(8,128)S(1)}, u32[]{:S(2)}) %copy-start.2) | copy-done | bytes 196632
  39.3 1.9 %shard_map.68 = (f32[3,8,16,128]{3,2,1,0:T(8,128)}, f32[3,8,16,128]{3,2,1,0:T(8,128)}, f32[3,8,16,128]{3,2,1,0:T(8,128)}) custom-call(f32[3,8,16,128]{3,2,1,0:T(8,128)} %copy-done, f32[3,8,16,128]{3,2,1,0:T(8,128)} %copy-done.1, f32[3,8,16,128]{3,2,1,0:T(8,128)} %copy-done.2), custom_call_target="tpu_custom_call" | custom-call | tf_op jit(solution)/shard_map/pallas_call | solution.py:458
Async XLA Ops:
  37.2 0.7 %copy-start = (f32[3,8,16,128]{3,2,1,0:T(8,128)}, f32[3,8,16,128]{3,2,1,0:T(8,128)S(1)}, u32[]{:S(2)}) copy-start(f32[3,8,16,128]{3,2,1,0:T(8,128)S(1)} %get-tuple-element.6.refs_0_) | copy-start | bytes 589828
  37.9 0.7 %copy-start.1 = (f32[3,8,16,128]{3,2,1,0:T(8,128)}, f32[3,8,16,128]{3,2,1,0:T(8,128)S(1)}, u32[]{:S(2)}) copy-start(f32[3,8,16,128]{3,2,1,0:T(8,128)S(1)} %get-tuple-element.7.refs_1_) | copy-start | bytes 589828
  38.6 0.7 %copy-start.2 = (f32[3,8,16,128]{3,2,1,0:T(8,128)}, f32[3,8,16,128]{3,2,1,0:T(8,128)S(1)}, u32[]{:S(2)}) copy-start(f32[3,8,16,128]{3,2,1,0:T(8,128)S(1)} %get-tuple-element.8.refs_2_) | copy-start | bytes 589828

commit v5 on v4

--- a/solution.py
+++ b/solution.py
@@ -61,7 +61,7 @@
 
 def kernel(counts, sol_hbm, res_hbm, den_hbm, fix_hbm, out_s, out_r, out_d, *scratch):
     n_rounds = len(ROUNDS)
-    sol, res, den, fix, load_sem = scratch[-5:]
+    sol, res, den, fix, load_sem, field, total_ref, mid_ref = scratch[-8:]
     loads = [
         pltpu.make_async_copy(src, dst, load_sem.at[i])
         for i, (src, dst) in enumerate(
@@ -75,11 +75,11 @@
     coef = rest[0:3]
     free_ref, diag_ref, inv_ref, fc0_ref, inv1_ref, inv2_ref = rest[3:9]
     part, send_sem, recv_sem, ssend_sem, srecv_sem = rest[9:14]
-    sums = rest[14:-5]
+    sums = rest[14:-8]
     groups = sum_groups(counts)
 
     idx = [lax.axis_index(a) for a in AXES]
-    ny, nz = den.shape[1:]
+    comps, nx, ny, nz = res.shape
     half = ny // 2
 
     barrier = pltpu.get_barrier_semaphore()
@@ -200,6 +200,56 @@
         planes = [roll(w, -2 * s * p, 1) for p in range(c * nx)]
         return jnp.stack(planes).reshape(c, nx, ny, nz)
 
+    def per_component(body):
+        lax.fori_loop(0, comps, lambda c, _: (body(c), None)[1], None)
+
+    def send_fine(r):
+        xs, _, ys, _, zs, _ = bufs[r]
+        xs[0] = field[:, nx - 1]
+        xs[1] = field[:, 0]
+        start(r, 0)
+        ys[0] = field[:, :, ny - 1 : ny]
+        ys[1] = field[:, :, 0:1]
+        start(r, 1)
+        place = ((iota((ny, nz), 1) + 1) % nz) // 2
+
+        def pack(c, packed):
+            part_c = jnp.zeros((ny, nz), jnp.float32)
+            for p in range(nx):
+                part_c = jnp.where(place == p, roll(field[c, p], 2 * p, 1), part_c)
+            return packed + pltpu.roll(part_c, lax.rem(2 * nx * c, nz), 1)
+
+        zs[...] = lax.fori_loop(0, comps, pack, jnp.zeros((ny, nz), jnp.float32))
+        start(r, 2)
+
+    def local_fine():
+        def body(c):
+            total_ref[c] = local_sum(0, field[pl.ds(c, 1)])[0]
+
+        per_component(body)
+
+    def halo_fine(r):
+        _, xr, _, yr, _, zr = bufs[r]
+        ref = coef[0]
+        sent_all(r - 1)
+        for a in range(3):
+            wait(r, a)
+        even = (iota((ny, nz), 1) & 1) == 0
+        beside = jnp.where(even, roll(zr[0], 1, 1), roll(zr[1], -1, 1))
+
+        def one(c):
+            w = pltpu.roll(beside, lax.rem(nz - 2 * nx * c, nz), 1)
+            z = jnp.stack([roll(w, -2 * p, 1) for p in range(nx)])
+            t = total_ref[c] + ref[7] * z
+            first = t[:1] + ref[0, 0:1] * xr[0, pl.ds(c, 1)]
+            last = t[nx - 1 :] + ref[1, nx - 1 : nx] * xr[1, pl.ds(c, 1)]
+            t = jnp.concatenate([first, t[1 : nx - 1], last], 0)
+            top = t[:, :half] + ref[6, :, :half] * yr[0, c]
+            bottom = t[:, half:] + ref[6, :, half:] * yr[1, c]
+            return jnp.concatenate([top, bottom], 1)
+
+        return one
+
     def set_coef(level, lows, ups):
         ref = coef[level]
         s = 2**level
@@ -300,15 +350,21 @@
     inv_ref[...] = 1.0 / diag_ref[...]
     fc0_ref[...] = damping * res[...] * inv_ref[...]
 
-    masked = free_ref[...] * fc0_ref[...]
-    send(1, masked, 1)
+    field[...] = free_ref[...] * fc0_ref[...]
+    send_fine(1)
     set_coef(0, lows, ups)
-    total = local_sum(0, masked)
+    local_fine()
     lows, ups = coarse_links(0, lows, ups)
     spring = restrict(spring, 1)
     inv1_ref[...] = 1.0 / diagonal(lows, ups, spring)
-    total = halo_sum(0, 1, total)
-    mid_rhs = restrict((1.0 - damping) * res[...] + free_ref[...] * total, 1)
+    neighbour_sum = halo_fine(1)
+
+    def first_residual(c):
+        left = (1.0 - damping) * res[c] + free_ref[c] * neighbour_sum(c)
+        mid_ref[c] = restrict(left, 1)
+
+    per_component(first_residual)
+    mid_rhs = mid_ref[...]
     mid0 = damping * mid_rhs * inv1_ref[...]
     send(2, mid0, 2)
     set_coef(1, lows, ups)
@@ -333,30 +389,49 @@
 
     mid = mid0 + prolong(iterate)
     mid = (1.0 - damping) * mid + mid0 + damping * neighbours(1, 5, mid) * inv1_ref[...]
-    fine = fc0_ref[...] + prolong(mid)
-    total = neighbours(0, 6, free_ref[...] * fine)
-    direction = (
-        (1.0 - damping) * fine + fc0_ref[...] + damping * free_ref[...] * total * inv_ref[...]
-    )
-    out_d[...] = direction
-    masked = free_ref[...] * direction
-    send(7, masked, 1)
+    mid_ref[...] = mid
+
+    def corrected(c):
+        return fc0_ref[c] + prolong(mid_ref[pl.ds(c, 1)])[0]
+
+    def mask_corrected(c):
+        field[c] = free_ref[c] * corrected(c)
+
+    per_component(mask_corrected)
+    send_fine(6)
+    local_fine()
+    neighbour_sum_2 = halo_fine(6)
+
+    def smooth(c):
+        change = damping * free_ref[c] * neighbour_sum_2(c) * inv_ref[c]
+        direction = (1.0 - damping) * corrected(c) + fc0_ref[c] + change
+        out_d[c] = direction
+        field[c] = free_ref[c] * direction
+
+    per_component(smooth)
+    send_fine(7)
+    local_fine()
+    neighbour_sum_3 = halo_fine(7)
+
+    def products(c, sums_so_far):
+        direction = out_d[c]
+        image = diag_ref[c] * direction - free_ref[c] * neighbour_sum_3(c)
+        out_r[c] = image
+        both = (res[c] * direction, direction * image)
+        return tuple(
+            old + jnp.sum(new.reshape(-1, 8, nz), axis=0) for old, new in zip(sums_so_far, both)
+        )
+
+    none = jnp.zeros((8, nz), jnp.float32)
 
     def fold(v):
-        w = jnp.sum(jnp.sum(v.reshape(-1, 8, nz), axis=0), axis=0, keepdims=True)
+        w = jnp.sum(v, axis=0, keepdims=True)
         return w + roll(w, nz // 2, 1)
 
-    precond = fold(res[...] * direction)
-    image = diag_ref[...] * direction
-    curve = fold(direction * image)
-    out_r[...] = image
-    total = halo_sum(0, 7, local_sum(0, masked)) * free_ref[...]
-    curve = curve - fold(out_d[...] * total)
-    out_r[...] = out_r[...] - total
+    precond, curve = (fold(v) for v in lax.fori_loop(0, comps, products, (none, none)))
     head = iota((1, nz), 1) < nz // 2
     mine = jnp.where(head, precond, curve)
 
-    sent = []
     for g, group in enumerate(groups):
         buf = sums[g]
         size = group_size(counts, group)
@@ -379,31 +454,24 @@
         hops = [hop(k, own) for k in range(1, size)]
         for h in hops:
             h.start()
+        for h in hops:
+            h.wait_send()
         for k in range(1, size):
             hop(k, partner(group, -k)[1]).wait_recv()
         mine = jnp.sum(buf[...], axis=0)
-        sent += hops
 
     def grand(keep):
         return jnp.sum(jnp.where(keep, mine, 0.0), axis=1, keepdims=True)
 
     alpha = grand(head) / grand(jnp.logical_not(head))
     loads[3].wait()
-    out_s[...] = sol[...] + alpha * out_d[...]
-    out_r[...] = res[...] - alpha * out_r[...]
-
-    for h in sent:
-        h.wait_send()
+
+    def advance(c):
+        out_s[c] = sol[c] + alpha * out_d[c]
+        out_r[c] = res[c] - alpha * out_r[c]
+
+    per_component(advance)
     sent_all(n_rounds - 1)
-
-
-def deliver(*refs):
-    sem = refs[-1]
-    moves = [pltpu.make_async_copy(refs[i], refs[3 + i], sem.at[i]) for i in range(3)]
-    for move in moves:
-        move.start()
-    for move in moves:
-        move.wait()
 
 
 def shards(counts, solution, residual, density_bins, fixed_dofs):
@@ -439,13 +507,16 @@
         pltpu.VMEM(density_bins.shape, jnp.int32),
         pltpu.VMEM(fixed_dofs.shape, jnp.int32),
         pltpu.SemaphoreType.DMA((4,)),
+        pltpu.VMEM(residual.shape, f32),
+        pltpu.VMEM(residual.shape, f32),
+        pltpu.VMEM((comps, nx // 2, ny, nz), f32),
     ]
     operands = [
         pltpu.with_memory_space_constraint(x, pltpu.HBM)
         for x in (solution, residual, density_bins, fixed_dofs)
     ]
     shape = jax.ShapeDtypeStruct(residual.shape, f32)
-    results = pl.pallas_call(
+    return pl.pallas_call(
         functools.partial(kernel, counts),
         out_shape=(shape, shape, shape),
         in_specs=[pl.BlockSpec(memory_space=pltpu.HBM)] * 4,
@@ -455,13 +526,6 @@
             collective_id=0, has_side_effects=True, vmem_limit_bytes=32 * 2**20
         ),
     )(*operands)
-    return pl.pallas_call(
-        deliver,
-        out_shape=(shape, shape, shape),
-        in_specs=[pl.BlockSpec(memory_space=pltpu.VMEM)] * 3,
-        out_specs=(pl.BlockSpec(memory_space=pltpu.HBM),) * 3,
-        scratch_shapes=[pltpu.SemaphoreType.DMA((3,))],
-    )(*results)
 
 
 def solution(mesh):

time: 41.4 us -> 41.6 us (level)
    pallas_call x1, Pallas kernels: 36.6 us -> 38.7 us  [shards(): pl.pallas_call(functools.partial(kernel, counts), out_shape=(shape, shape...]
    pallas_call x1 -> x0, Pallas kernels: 1.94 us -> none  [shards(): pl.pallas_call(deliver, out_shape=(shape, shape, shape), in_specs=[pl.Blo...]
    unnamed x6 -> x3, local copies, waits for them, and re-layouts: 2.02 us -> 2.03 us
where the time goes in v5:
time: 41.6 us; the launch traced here: 41.4 us
  Pallas kernels  38.7 us (93%)
  local copies, waits for them, and re-layouts  2.03 us (5%)
  between operations  0.64 us (2%)
    pallas_call x1, Pallas kernels, shards(): pl.pallas_call(functools.partial(kernel, counts), out_shape=(shape, shape...  38.7 us
    unnamed x3, local copies, waits for them, and re-layouts  2.03 us

profile of v5, /device:TPU:0, one launch (start us, length us, event | category | flops | bytes accessed | tf_op | source)
XLA Modules:
  0.0 41.4 jit_solution(5728626155220572316)
XLA Ops:
  0.6 38.7 %shard_map.67 = (f32[3,8,16,128]{3,2,1,0:T(8,128)S(1)}, f32[3,8,16,128]{3,2,1,0:T(8,128)S(1)}, f32[3,8,16,128]{3,2,1,0:T(8,128)S(1)}) custom-call(f32[3,8,16,128]{3,2,1,0:T(8,128)} %sol_hbm.1, f32[3,8,16,128]{3,2,1,0:T(8,128)} %res_hbm.1, s32[8,16,128]{2,1,0:T(8,128)} %den_hbm.1, s32[3,8,16,128]{3,2,1,0:T(8,128)} %fix_hbm.1), custom_call_target="tpu_custom_call" | custom-call | tf_op jit(solution)/shard_map/pallas_call | solution.py:519
  39.4 0.7 %copy.10 = f32[3,8,16,128]{3,2,1,0:T(8,128)} copy(f32[3,8,16,128]{3,2,1,0:T(8,128)S(1)} %get-tuple-element.6) | data formatting | bytes 393216
  40.1 0.7 %copy.11 = f32[3,8,16,128]{3,2,1,0:T(8,128)} copy(f32[3,8,16,128]{3,2,1,0:T(8,128)S(1)} %get-tuple-element.7) | data formatting | bytes 393216
  40.7 0.7 %copy.12 = f32[3,8,16,128]{3,2,1,0:T(8,128)} copy(f32[3,8,16,128]{3,2,1,0:T(8,128)S(1)} %get-tuple-element.8) | data formatting | bytes 393216

commit v6 on v4

--- a/solution.py
+++ b/solution.py
@@ -59,13 +59,13 @@
     return size
 
 
-def kernel(counts, sol_hbm, res_hbm, den_hbm, fix_hbm, out_s, out_r, out_d, *scratch):
+def kernel(counts, res_hbm, den_hbm, fix_hbm, out_r, out_b, out_c, out_a, *scratch):
     n_rounds = len(ROUNDS)
-    sol, res, den, fix, load_sem = scratch[-5:]
+    res, den, fix, load_sem = scratch[-4:]
     loads = [
         pltpu.make_async_copy(src, dst, load_sem.at[i])
         for i, (src, dst) in enumerate(
-            ((den_hbm, den), (res_hbm, res), (fix_hbm, fix), (sol_hbm, sol))
+            ((den_hbm, den), (res_hbm, res), (fix_hbm, fix))
         )
     ]
     for load in loads:
@@ -75,7 +75,7 @@
     coef = rest[0:3]
     free_ref, diag_ref, inv_ref, fc0_ref, inv1_ref, inv2_ref = rest[3:9]
     part, send_sem, recv_sem, ssend_sem, srecv_sem = rest[9:14]
-    sums = rest[14:-5]
+    sums = rest[14:-4]
     groups = sum_groups(counts)
 
     idx = [lax.axis_index(a) for a in AXES]
@@ -335,10 +335,11 @@
     mid = (1.0 - damping) * mid + mid0 + damping * neighbours(1, 5, mid) * inv1_ref[...]
     fine = fc0_ref[...] + prolong(mid)
     total = neighbours(0, 6, free_ref[...] * fine)
-    direction = (
-        (1.0 - damping) * fine + fc0_ref[...] + damping * free_ref[...] * total * inv_ref[...]
-    )
-    out_d[...] = direction
+    base = (1.0 - damping) * fine + fc0_ref[...]
+    change = damping * free_ref[...] * total * inv_ref[...]
+    out_b[...] = base
+    out_c[...] = change
+    direction = base + change
     masked = free_ref[...] * direction
     send(7, masked, 1)
 
@@ -351,12 +352,13 @@
     curve = fold(direction * image)
     out_r[...] = image
     total = halo_sum(0, 7, local_sum(0, masked)) * free_ref[...]
-    curve = curve - fold(out_d[...] * total)
+    curve = curve - fold((out_b[...] + out_c[...]) * total)
     out_r[...] = out_r[...] - total
     head = iota((1, nz), 1) < nz // 2
     mine = jnp.where(head, precond, curve)
 
-    sent = []
+    sent_all(n_rounds - 1)
+
     for g, group in enumerate(groups):
         buf = sums[g]
         size = group_size(counts, group)
@@ -379,31 +381,17 @@
         hops = [hop(k, own) for k in range(1, size)]
         for h in hops:
             h.start()
+        for h in hops:
+            h.wait_send()
         for k in range(1, size):
             hop(k, partner(group, -k)[1]).wait_recv()
         mine = jnp.sum(buf[...], axis=0)
-        sent += hops
 
     def grand(keep):
         return jnp.sum(jnp.where(keep, mine, 0.0), axis=1, keepdims=True)
 
     alpha = grand(head) / grand(jnp.logical_not(head))
-    loads[3].wait()
-    out_s[...] = sol[...] + alpha * out_d[...]
-    out_r[...] = res[...] - alpha * out_r[...]
-
-    for h in sent:
-        h.wait_send()
-    sent_all(n_rounds - 1)
-
-
-def deliver(*refs):
-    sem = refs[-1]
-    moves = [pltpu.make_async_copy(refs[i], refs[3 + i], sem.at[i]) for i in range(3)]
-    for move in moves:
-        move.start()
-    for move in moves:
-        move.wait()
+    out_a[...] = jnp.broadcast_to(alpha, out_a.shape)
 
 
 def shards(counts, solution, residual, density_bins, fixed_dofs):
@@ -434,34 +422,28 @@
     ]
     scratch += [pltpu.VMEM((size, 1, nz), f32) for size in sizes]
     scratch += [
-        pltpu.VMEM(solution.shape, f32),
         pltpu.VMEM(residual.shape, f32),
         pltpu.VMEM(density_bins.shape, jnp.int32),
         pltpu.VMEM(fixed_dofs.shape, jnp.int32),
-        pltpu.SemaphoreType.DMA((4,)),
+        pltpu.SemaphoreType.DMA((3,)),
     ]
     operands = [
         pltpu.with_memory_space_constraint(x, pltpu.HBM)
-        for x in (solution, residual, density_bins, fixed_dofs)
+        for x in (residual, density_bins, fixed_dofs)
     ]
     shape = jax.ShapeDtypeStruct(residual.shape, f32)
-    results = pl.pallas_call(
+    image, base, change, alpha = pl.pallas_call(
         functools.partial(kernel, counts),
-        out_shape=(shape, shape, shape),
-        in_specs=[pl.BlockSpec(memory_space=pltpu.HBM)] * 4,
-        out_specs=(pl.BlockSpec(memory_space=pltpu.VMEM),) * 3,
+        out_shape=(shape, shape, shape, jax.ShapeDtypeStruct((1, nz), f32)),
+        in_specs=[pl.BlockSpec(memory_space=pltpu.HBM)] * 3,
+        out_specs=(pl.BlockSpec(memory_space=pltpu.VMEM),) * 4,
         scratch_shapes=scratch,
         compiler_params=pltpu.CompilerParams(
             collective_id=0, has_side_effects=True, vmem_limit_bytes=32 * 2**20
         ),
     )(*operands)
-    return pl.pallas_call(
-        deliver,
-        out_shape=(shape, shape, shape),
-        in_specs=[pl.BlockSpec(memory_space=pltpu.VMEM)] * 3,
-        out_specs=(pl.BlockSpec(memory_space=pltpu.HBM),) * 3,
-        scratch_shapes=[pltpu.SemaphoreType.DMA((3,))],
-    )(*results)
+    direction = base + change
+    return (solution + alpha * direction, residual - alpha * image, direction)
 
 
 def solution(mesh):

time: 41.4 us -> 38.2 us (0.923)
  Pallas kernels: 38.6 us -> 36.5 us
  local copies, waits for them, and re-layouts: 2.02 us -> 0.01 us
  other arithmetic: 0 us -> 0.86 us
    unnamed x6 -> x4, local copies, waits for them, and re-layouts: 2.02 us -> 0.01 us
    pallas_call x1 -> x0, Pallas kernels: 1.94 us -> none  [shards(): pl.pallas_call(deliver, out_shape=(shape, shape, shape), in_specs=[pl.Blo...]
    add x0 -> x1, other arithmetic: none -> 0.86 us  [shards(): return (solution + alpha * direction, residual - alpha * image, direction)]
where the time goes in v6:
time: 38.2 us; the launch traced here: 38 us
  Pallas kernels  36.5 us (96%)
  other arithmetic  0.86 us (2%)
  between operations  0.67 us (2%)
    pallas_call x1, Pallas kernels, shards(): pl.pallas_call(functools.partial(kernel, counts), out_shape=(shape, shape...  36.5 us
    add x1, other arithmetic, shards(): return (solution + alpha * direction, residual - alpha * image, direction)  0.86 us

profile of v6, /device:TPU:0, one launch (start us, length us, event | category | flops | bytes accessed | tf_op | source)
XLA Modules:
  0.0 38.0 jit_solution(11111868922131251946)
XLA Ops:
  0.6 0.0 copy-start
  0.6 0.0 copy-start.1
  0.7 36.5 %shard_map.67 = (f32[3,8,16,128]{3,2,1,0:T(8,128)S(1)}, f32[3,8,16,128]{3,2,1,0:T(8,128)S(1)}, f32[3,8,16,128]{3,2,1,0:T(8,128)S(1)}, f32[1,128]{1,0:T(1,128)S(1)}) custom-call(f32[3,8,16,128]{3,2,1,0:T(8,128)} %res_hbm.1, s32[8,16,128]{2,1,0:T(8,128)} %den_hbm.1, s32[3,8,16,128]{3,2,1,0:T(8,128)} %fix_hbm.1), custom_call_target="tpu_custom_call" | custom-call | tf_op jit(solution)/shard_map/pallas_call | solution.py:435
  37.2 0.0 copy-done
  37.2 0.0 copy-done.1
  37.2 0.9 %multiply_add_fusion = (f32[3,8,16,128]{3,2,1,0:T(8,128)}, f32[3,8,16,128]{3,2,1,0:T(8,128)}, f32[3,8,16,128]{3,2,1,0:T(8,128)}) fusion(f32[3,8,16,128]{3,2,1,0:T(8,128)S(1)} %copy-done.1, f32[128]{0:T(128)S(1)} %bitcast.1, f32[3,8,16,128]{3,2,1,0:T(8,128)S(1)} %get-tuple-element.8, f32[3,8,16,128]{3,2,1,0:T(8,128)S(1)} %get-tuple-element.9, ...), kind=kLoop, calls=%fused_computation.1 | loop fusion | flops 245760 | bytes 1573376 | tf_op jit(solution)/shard_map/add | solution.py:446
Async XLA Ops:
  0.6 36.5 %copy-start = (f32[3,8,16,128]{3,2,1,0:T(8,128)S(1)}, f32[3,8,16,128]{3,2,1,0:T(8,128)}, u32[]{:S(2)}) copy-start(f32[3,8,16,128]{3,2,1,0:T(8,128)} %res_hbm.1) | copy-start | bytes 589828
  0.6 36.5 %copy-start.1 = (f32[3,8,16,128]{3,2,1,0:T(8,128)S(1)}, f32[3,8,16,128]{3,2,1,0:T(8,128)}, u32[]{:S(2)}) copy-start(f32[3,8,16,128]{3,2,1,0:T(8,128)} %param.4) | copy-start | bytes 589828

commit v7 on v6

--- a/solution.py
+++ b/solution.py
@@ -181,20 +181,23 @@
         else:
             xs[0, 0] = share(v[:, nx - 1])
             xs[1, 0] = share(v[:, 0])
-        start(r, 0)
         ys[0] = v[:, :, ny - 1 : ny]
         ys[1] = v[:, :, 0:1]
-        start(r, 1)
+        if s == 1:
+            start(r, 0)
+            start(r, 1)
         place = ((iota((ny, nz), 1) + s) % nz) // (2 * s)
         packed = jnp.zeros((ny, nz), jnp.float32)
         for p in range(c * nx):
             packed = jnp.where(place == p, roll(v[p // nx, p % nx], 2 * s * p, 1), packed)
         zs[...] = packed
         start(r, 2)
+        if s > 1:
+            start(r, 0)
+            start(r, 1)
 
     def z_halo(r, s, c, nx):
         zr = bufs[r][5]
-        wait(r, 2)
         even = (iota((ny, nz), 1) & s) == 0
         w = jnp.where(even, roll(zr[0], s, 1), roll(zr[1], -s, 1))
         planes = [roll(w, -2 * s * p, 1) for p in range(c * nx)]
@@ -229,13 +232,13 @@
         _, xr, _, yr, _, _ = bufs[r]
         nx = total.shape[1]
         sent_all(r - 1)
-        wait(r, 0)
+        for a in range(3):
+            wait(r, a)
         faces = [xr[i][:, None] if s == 1 else unshare(xr[i, 0], total.shape[0]) for i in (0, 1)]
         first = total[:, :1] + ref[0, 0:1] * faces[0]
         last = total[:, nx - 1 :] + ref[1, nx - 1 : nx] * faces[1]
         middle = [total[:, 1 : nx - 1]] if nx > 2 else []
         total = jnp.concatenate([first] + middle + [last], 1)
-        wait(r, 1)
         top = total[:, :, :half] + ref[6, :, :half] * yr[0]
         bottom = total[:, :, half:] + ref[6, :, half:] * yr[1]
         total = jnp.concatenate([top, bottom], 2)
@@ -281,10 +284,10 @@
     def shared(other):
         return jnp.where(other > 0.0, 0.5 * (modulus + other), 0.0)
 
-    wait(0, 0)
+    for a in range(3):
+        wait(0, a)
     lows = [shared(jnp.concatenate([xr[0], modulus[:-1]], 0))]
     ups = [shared(jnp.concatenate([modulus[1:], xr[1]], 0))]
-    wait(0, 1)
     lows.append(shared(jnp.where(row == 0, yr[0, 0], roll(modulus, 1, 1))))
     ups.append(shared(jnp.where(row == ny - 1, yr[1, 0], roll(modulus, -1, 1))))
     beside = z_halo(0, 1, 1, modulus.shape[0])[0]

time: 38.2 us -> 38.1 us (level)
  no operation moved by 1% of the time
where the time goes in v7:
time: 38.1 us; the launch traced here: 38 us
  Pallas kernels  36.5 us (96%)
  other arithmetic  0.86 us (2%)
  between operations  0.67 us (2%)
    pallas_call x1, Pallas kernels, shards(): pl.pallas_call(functools.partial(kernel, counts), out_shape=(shape, shape...  36.5 us
    add x1, other arithmetic, shards(): return (solution + alpha * direction, residual - alpha * image, direction)  0.86 us

profile of v7, /device:TPU:0, one launch (start us, length us, event | category | flops | bytes accessed | tf_op | source)
XLA Modules:
  0.0 38.0 jit_solution(1729089625328785735)
XLA Ops:
  0.6 0.0 copy-start
  0.6 0.0 copy-start.1
  0.7 36.5 %shard_map.67 = (f32[3,8,16,128]{3,2,1,0:T(8,128)S(1)}, f32[3,8,16,128]{3,2,1,0:T(8,128)S(1)}, f32[3,8,16,128]{3,2,1,0:T(8,128)S(1)}, f32[1,128]{1,0:T(1,128)S(1)}) custom-call(f32[3,8,16,128]{3,2,1,0:T(8,128)} %res_hbm.1, s32[8,16,128]{2,1,0:T(8,128)} %den_hbm.1, s32[3,8,16,128]{3,2,1,0:T(8,128)} %fix_hbm.1), custom_call_target="tpu_custom_call" | custom-call | tf_op jit(solution)/shard_map/pallas_call | solution.py:438
  37.1 0.0 copy-done
  37.1 0.0 copy-done.1
  37.1 0.9 %multiply_add_fusion = (f32[3,8,16,128]{3,2,1,0:T(8,128)}, f32[3,8,16,128]{3,2,1,0:T(8,128)}, f32[3,8,16,128]{3,2,1,0:T(8,128)}) fusion(f32[3,8,16,128]{3,2,1,0:T(8,128)S(1)} %copy-done.1, f32[128]{0:T(128)S(1)} %bitcast.1, f32[3,8,16,128]{3,2,1,0:T(8,128)S(1)} %get-tuple-element.8, f32[3,8,16,128]{3,2,1,0:T(8,128)S(1)} %get-tuple-element.9, ...), kind=kLoop, calls=%fused_computation.1 | loop fusion | flops 245760 | bytes 1573376 | tf_op jit(solution)/shard_map/add | solution.py:449
Async XLA Ops:
  0.6 36.5 %copy-start = (f32[3,8,16,128]{3,2,1,0:T(8,128)S(1)}, f32[3,8,16,128]{3,2,1,0:T(8,128)}, u32[]{:S(2)}) copy-start(f32[3,8,16,128]{3,2,1,0:T(8,128)} %res_hbm.1) | copy-start | bytes 589828
  0.6 36.5 %copy-start.1 = (f32[3,8,16,128]{3,2,1,0:T(8,128)S(1)}, f32[3,8,16,128]{3,2,1,0:T(8,128)}, u32[]{:S(2)}) copy-start(f32[3,8,16,128]{3,2,1,0:T(8,128)} %param.4) | copy-start | bytes 589828

commit v8 on v7

--- a/solution.py
+++ b/solution.py
@@ -49,7 +49,7 @@
 
 def sum_groups(counts):
     total = counts[0] * counts[1] * counts[2]
-    return ((0, 1, 2),) if total <= 64 else ((2,), (1,), (0,))
+    return ((1, 2), (0,)) if total <= 64 else ((2,), (1,), (0,))
 
 
 def group_size(counts, group):

time: 38.1 us -> 39 us (1.024)
  Pallas kernels: 36.5 us -> 37.3 us
    pallas_call x1, Pallas kernels: 36.5 us -> 37.3 us  [shards(): pl.pallas_call(functools.partial(kernel, counts), out_shape=(shape, shape...]
where the time goes in v8:
time: 39 us; the launch traced here: 38.8 us
  Pallas kernels  37.3 us (96%)
  other arithmetic  0.86 us (2%)
  between operations  0.67 us (2%)
    pallas_call x1, Pallas kernels, shards(): pl.pallas_call(functools.partial(kernel, counts), out_shape=(shape, shape...  37.3 us
    add x1, other arithmetic, shards(): return (solution + alpha * direction, residual - alpha * image, direction)  0.86 us

profile of v8, /device:TPU:0, one launch (start us, length us, event | category | flops | bytes accessed | tf_op | source)
XLA Modules:
  0.0 38.8 jit_solution(13530234510259544549)
XLA Ops:
  0.6 0.0 copy-start
  0.6 0.0 copy-start.1
  0.7 37.3 %shard_map.67 = (f32[3,8,16,128]{3,2,1,0:T(8,128)S(1)}, f32[3,8,16,128]{3,2,1,0:T(8,128)S(1)}, f32[3,8,16,128]{3,2,1,0:T(8,128)S(1)}, f32[1,128]{1,0:T(1,128)S(1)}) custom-call(f32[3,8,16,128]{3,2,1,0:T(8,128)} %res_hbm.1, s32[8,16,128]{2,1,0:T(8,128)} %den_hbm.1, s32[3,8,16,128]{3,2,1,0:T(8,128)} %fix_hbm.1), custom_call_target="tpu_custom_call" | custom-call | tf_op jit(solution)/shard_map/pallas_call | solution.py:438
  37.9 0.0 copy-done
  37.9 0.0 copy-done.1
  38.0 0.9 %multiply_add_fusion = (f32[3,8,16,128]{3,2,1,0:T(8,128)}, f32[3,8,16,128]{3,2,1,0:T(8,128)}, f32[3,8,16,128]{3,2,1,0:T(8,128)}) fusion(f32[3,8,16,128]{3,2,1,0:T(8,128)S(1)} %copy-done.1, f32[128]{0:T(128)S(1)} %bitcast.1, f32[3,8,16,128]{3,2,1,0:T(8,128)S(1)} %get-tuple-element.8, f32[3,8,16,128]{3,2,1,0:T(8,128)S(1)} %get-tuple-element.9, ...), kind=kLoop, calls=%fused_computation.1 | loop fusion | flops 245760 | bytes 1573376 | tf_op jit(solution)/shard_map/add | solution.py:449
Async XLA Ops:
  0.6 37.3 %copy-start = (f32[3,8,16,128]{3,2,1,0:T(8,128)S(1)}, f32[3,8,16,128]{3,2,1,0:T(8,128)}, u32[]{:S(2)}) copy-start(f32[3,8,16,128]{3,2,1,0:T(8,128)} %res_hbm.1) | copy-start | bytes 589828
  0.6 37.3 %copy-start.1 = (f32[3,8,16,128]{3,2,1,0:T(8,128)S(1)}, f32[3,8,16,128]{3,2,1,0:T(8,128)}, u32[]{:S(2)}) copy-start(f32[3,8,16,128]{3,2,1,0:T(8,128)} %param.4) | copy-start | bytes 589828
